TPU v7x, 512 devices: a whole 4x4x16 slice. The times are simulated.
512 devices in a mesh: ex: 32 (over z, core), fsdp: 16 (over y, x).
Axes of the slice: x: 4, y: 4, z: 16, core: 2. Of those that a mesh axis runs over, the one named last changes fastest.
Arguments:
- train_inputs: bfloat16 [512, 128, 5120], P(('ex', 'fsdp')), may hold values from -6 to 6
- train_upstream: bfloat16 [512, 128, 5120], P(('ex', 'fsdp')), may hold values from -6 to 6
- held_inputs: bfloat16 [128, 128, 5120], P('ex', 'fsdp'), may hold values from -6 to 6
- held_upstream: bfloat16 [128, 128, 5120], P('ex', 'fsdp'), may hold values from -6 to 6
- adapter_down: bfloat16 [5120, 128], P('fsdp'), may hold values from -0.078125 to 0.078125
- adapter_up: bfloat16 [128, 5120], P(None, 'fsdp'), may hold values from -0.5 to 0.5
- rank_signs_up: bfloat16 [128, 64], replicated, may hold values from -1 to 1, as said below
- rank_signs_down: bfloat16 [128, 64], replicated, may hold values from -1 to 1, as said below
- width_signs_up: bfloat16 [5120, 64], P('fsdp'), may hold values from -1 to 1, as said below
- width_signs_down: bfloat16 [5120, 64], P('fsdp'), may hold values from -1 to 1, as said below
Outputs:
- train_features: bfloat16 [512, 8192], P(('ex', 'fsdp'))
- influence: float32 [512, 128], P(('ex', 'fsdp'))
Inputs may be any that keep to these rules, and one draw needn't show every extreme that they name: `rank_signs_up`: every entry is +1 or -1. `rank_signs_down`: every entry is +1 or -1. `width_signs_up`: every entry is +1 or -1. `width_signs_down`: every entry is +1 or -1.
All inputs are finite; a program needn't handle non-finite values.
Results may differ from a plain program's by a relative error of at most 0.0033.
Values may be sent and summed in bfloat16 or wider, within the bound.
No kernel may reach another device: no remote copies, remote signals or barrier semaphores. Data moves between devices by JAX's collectives and lax.ppermute only.
A program may use at most 64 MiB of HBM per device.

v0:
```python
import math

import jax
import jax.numpy as jnp
from jax import lax
from jax.sharding import PartitionSpec as P

EPSILON = 1e-06
HIGH = lax.Precision.HIGHEST


def scaled(values):
    return values * lax.rsqrt(jnp.mean(values * values, axis=1, keepdims=True) + EPSILON)


def explicit_terms(inputs, upstream, down_full, up_full, rank_up, rank_down, wide_up, wide_down):
    hidden = jnp.einsum("esd,dr->esr", inputs, down_full, preferred_element_type=jnp.float32)
    mapped = jnp.einsum("esd,rd->esr", upstream, up_full, preferred_element_type=jnp.float32)
    grad_up = jnp.einsum("esr,esd->erd", hidden, upstream.astype(jnp.float32), precision=HIGH)
    grad_down = jnp.einsum("esr,esd->erd", mapped, inputs.astype(jnp.float32), precision=HIGH)
    side_up = jnp.einsum("rk,erd->ekd", rank_up, grad_up, precision=HIGH)
    side_down = jnp.einsum("rk,erd->ekd", rank_down, grad_down, precision=HIGH)
    block_up = jnp.einsum("ekd,dm->ekm", side_up, wide_up, precision=HIGH)
    block_down = jnp.einsum("ekd,dm->ekm", side_down, wide_down, precision=HIGH)
    return jnp.stack([block_up, block_down], axis=1).reshape(inputs.shape[0], -1)


def shards(
    train_inputs,
    train_upstream,
    held_inputs,
    held_upstream,
    adapter_down,
    adapter_up,
    rank_signs_up,
    rank_signs_down,
    width_signs_up,
    width_signs_down,
):
    wide_up, wide_down = (
        lax.all_gather(width_signs_up, "fsdp", axis=0, tiled=True),
        lax.all_gather(width_signs_down, "fsdp", axis=0, tiled=True),
    )
    down_full, up_full = (
        lax.all_gather(adapter_down, "fsdp", axis=0, tiled=True),
        lax.all_gather(adapter_up, "fsdp", axis=1, tiled=True),
    )
    rank_up = rank_signs_up.astype(jnp.float32)
    rank_down = rank_signs_down.astype(jnp.float32)
    wide_up_full = wide_up.astype(jnp.float32)
    wide_down_full = wide_down.astype(jnp.float32)
    train_part = explicit_terms(
        train_inputs,
        train_upstream,
        down_full,
        up_full,
        rank_up,
        rank_down,
        wide_up_full,
        wide_down_full,
    )
    held_part = explicit_terms(
        held_inputs,
        held_upstream,
        down_full,
        up_full,
        rank_up,
        rank_down,
        wide_up_full,
        wide_down_full,
    )
    train_features = scaled(train_part).astype(jnp.bfloat16)
    total_width = held_part.shape[1]
    held_total = lax.psum(held_part, "fsdp")
    held_features = scaled(held_total).astype(jnp.bfloat16)
    held_every = lax.all_gather(held_features, "ex", axis=0, tiled=True)
    influence = jnp.einsum(
        "tn,vn->tv", train_features, held_every, preferred_element_type=jnp.float32
    ) / math.sqrt(total_width)
    return (train_features, influence)


def solution(mesh):
    placed = (
        P(("ex", "fsdp"), None, None),
        P(("ex", "fsdp"), None, None),
        P("ex", "fsdp", None),
        P("ex", "fsdp", None),
        P("fsdp", None),
        P(None, "fsdp"),
        P(),
        P(),
        P("fsdp", None),
        P("fsdp", None),
    )
    return jax.shard_map(
        shards,
        mesh=mesh,
        in_specs=placed,
        out_specs=(P(("ex", "fsdp"), None), P(("ex", "fsdp"), None)),
        check_vma=False,
    )
```

profile of v0, /device:TPU:1, one launch (start us, length us, event | category | flops | bytes accessed | tf_op | source)
XLA Modules:
  0.0 355.9 jit_solution(14298590953622649248)
XLA Ops:
  7.2 0.7 all-gather.7.cloned.1.call-update
  8.0 0.7 all-gather.9.cloned.1.call-update
  8.7 20.7 %all-gather = bf16[16,320,64]{1,2,0:T(8,128)(2,1)S(1)} all-gather(bf16[1,320,64]{1,2,0:T(8,128)(2,1)} %bitcast.98), channel_id=1, replica_groups=mesh['ex'=32,'fsdp'=16] {'fsdp'}, dimensions={0}, use_global_device_ids=true | all-gather | bytes 696320 | tf_op jit(solution)/shard_map/all_gather | solution.py:41
  29.9 1.5 reshape.127
  31.4 18.8 %all-gather.1 = bf16[16,320,64]{1,2,0:T(8,128)(2,1)S(1)} all-gather(bf16[1,320,64]{1,2,0:T(8,128)(2,1)S(1)} %bitcast.99), channel_id=1, replica_groups=mesh['ex'=32,'fsdp'=16] {'fsdp'}, dimensions={0}, use_global_device_ids=true | all-gather | bytes 696320 | tf_op jit(solution)/shard_map/all_gather | solution.py:42
  50.7 0.6 reshape.130
  51.3 22.9 %all-gather.7.cloned.1.call-done = bf16[5120,128]{1,0:T(8,128)(2,1)} async-done(((bf16[320,128]{1,0:T(8,128)(2,1)}), bf16[5120,128]{1,0:T(8,128)(2,1)}) %all-gather.7.cloned.1.call-update) | async-done | bytes 1310736 | tf_op jit(solution)/shard_map/all_gather | solution.py:45
  74.2 1.8 fusion.2
  76.0 6.9 %fusion.17 = f32[4,128,5120]{2,1,0:T(8,128)} fusion(f32[4,8,128]{2,1,0:T(8,128)S(1)} %fusion.2, bf16[4,8,5120]{2,1,0:T(8,128)(2,1)S(1)} %copy-done.5), kind=kOutput, calls=%fused_computation.33 | convolution fusion | flops 251658240 | bytes 10829824 | tf_op jit(solution)/shard_map/esr,esd->erd/dot_general | solution.py:19
  82.9 52.5 %all-gather.9.cloned.1.call-done = bf16[128,5120]{0,1:T(8,128)(2,1)} async-done(((bf16[128,320]{0,1:T(8,128)(2,1)}), bf16[128,5120]{0,1:T(8,128)(2,1)}) %all-gather.9.cloned.1.call-update) | async-done | bytes 1310736 | tf_op jit(solution)/shard_map/all_gather | solution.py:46
  135.4 1.8 fusion
  137.2 4.3 %fusion.18 = f32[4,128,5120]{2,1,0:T(8,128)S(1)} fusion(f32[4,8,128]{2,1,0:T(8,128)S(1)} %fusion, bf16[4,8,5120]{2,1,0:T(8,128)(2,1)S(1)} %copy-done.6), kind=kOutput, calls=%fused_computation.34 | convolution fusion | flops 251658240 | bytes 10829824 | tf_op jit(solution)/shard_map/esr,esd->erd/dot_general | solution.py:20
  141.5 5.0 %convolution_bitcast_fusion.1 = f32[4,64,5120]{2,1,0:T(8,128)S(1)} fusion(f32[4,128,5120]{2,1,0:T(8,128)S(1)} %copy-done.1, bf16[128,64]{0,1:T(8,128)(2,1)S(1)} %copy-done.7), kind=kOutput, calls=%fused_computation.1 | convolution fusion | flops 2013265920 | bytes 15745024 | tf_op jit(solution)/shard_map/rk,erd->ekd/dot_general | solution.py:21
  146.5 2.5 convolution_bitcast_fusion.5
  149.0 5.2 %convolution_bitcast_fusion = f32[4,64,5120]{2,1,0:T(8,128)S(1)} fusion(f32[4,128,5120]{2,1,0:T(8,128)S(1)} %fusion.18, bf16[128,64]{0,1:T(8,128)(2,1)S(1)} %copy-done.8), kind=kOutput, calls=%fused_computation | convolution fusion | flops 2013265920 | bytes 15745024 | tf_op jit(solution)/shard_map/rk,erd->ekd/dot_general | solution.py:22
  154.2 2.5 convolution_bitcast_fusion.4
  156.7 0.8 reshape.118
  157.6 111.9 %all-reduce.2.cloned.1.call-done = f32[4,8192]{1,0:T(4,128)} async-done(((f32[4,8192]{1,0:T(4,128)}), f32[4,8192]{1,0:T(4,128)}) %all-reduce.2.cloned.1.call-update) | async-done | bytes 131088 | tf_op jit(solution)/shard_map/psum | solution.py:74
  269.5 1.1 multiply_reduce_fusion
  270.5 1.6 fusion.14
  273.5 2.2 fusion.10
  275.7 1.2 fusion.6
  276.9 1.1 convolution_bitcast_fusion.3
  278.1 0.7 convolution_bitcast_fusion.7
  279.9 0.8 copy-done.2
  280.7 1.2 fusion.8
  281.9 1.1 convolution_bitcast_fusion.2
  283.1 0.7 convolution_bitcast_fusion.6
  285.2 0.7 convert_element_type.30
  286.0 59.7 %all-gather.11.cloned.1.call-done = bf16[32,4,8192]{2,1,0:T(4,128)(2,1)} async-done(((bf16[1,4,8192]{2,1,0:T(4,128)(2,1)}), bf16[32,4,8192]{2,1,0:T(4,128)(2,1)}) %all-gather.11.cloned.1.call-update) | async-done | bytes 2097168 | tf_op jit(solution)/shard_map/all_gather | solution.py:76
  345.6 2.5 reshape.124
  348.2 1.2 fusion.13
  (38 shorter events, 4.2 us)
Async XLA Ops:
  7.2 268.5 %copy-start = (bf16[1,128,5120]{2,1,0:T(8,128)(2,1)S(1)}, bf16[1,128,5120]{2,1,0:T(8,128)(2,1)}, u32[]{:S(2)}) copy-start(bf16[1,128,5120]{2,1,0:T(8,128)(2,1)} %param.11) | copy-start | bytes 3932164
  7.2 67.0 %all-gather.7.cloned.1.call-start = ((), (), s32[]{:S(2)}) async-start(), calls=%async_computation | async-start | bytes 1392640 | tf_op jit(solution)/shard_map/all_gather | solution.py:45
  7.9 127.5 %all-gather.9.cloned.1.call-start = ((), (), s32[]{:S(2)}) async-start(), calls=%async_computation.1 | async-start | bytes 1392640 | tf_op jit(solution)/shard_map/all_gather | solution.py:46
  8.7 260.8 %all-reduce.2.cloned.1.call-start = ((), (), s32[]{:S(2)}) async-start(), calls=%async_computation.2 | async-start | bytes 262144 | tf_op jit(solution)/shard_map/psum | solution.py:74
  29.4 2.0 copy-start.10
  74.2 1.8 copy-start.5
  135.4 1.8 copy-start.6
  137.2 4.3 %copy-start.1 = (f32[4,128,5120]{2,1,0:T(8,128)S(1)}, f32[4,128,5120]{2,1,0:T(8,128)}, u32[]{:S(2)}) copy-start(f32[4,128,5120]{2,1,0:T(8,128)} %fusion.17) | copy-start | bytes 31457284
  137.2 4.3 %copy-start.7 = (bf16[128,64]{0,1:T(8,128)(2,1)S(1)}, bf16[128,64]{0,1:T(8,128)(2,1)}, u32[]{:S(2)}) copy-start(bf16[128,64]{0,1:T(8,128)(2,1)} %param.16) | copy-start | bytes 49156
  141.5 5.0 %copy-start.4 = (bf16[5120,64,1]{0,1,2:T(8,128)(2,1)S(1)}, bf16[5120,64,1]{0,1,2:T(8,128)(2,1)}, u32[]{:S(2)}) copy-start(bf16[5120,64,1]{0,1,2:T(8,128)(2,1)} %reshape.127) | copy-start | bytes 1966084
  146.5 2.5 copy-start.8
  157.6 188.1 %all-gather.11.cloned.1.call-start = ((), (), s32[]{:S(2)}) async-start(), calls=%async_computation.3 | async-start | bytes 2162688 | tf_op jit(solution)/shard_map/all_gather | solution.py:76
  278.1 1.3 copy-start.3
  279.4 1.3 copy-start.2
  280.7 1.2 copy-start.9
Sparse Core Ops, SparseCore 0:
  11.0 63.1 all-gather.6
  77.2 58.1 all-gather.8
  157.7 111.7 all-reduce.1
  272.3 73.2 all-gather.10
where the time goes:
time: 356 us
  waiting for transfers between devices  248 us (70%)
  matrix products  39.8 us (11%)
  blocking collectives  39.5 us (11%)
  between operations  14.8 us (4%)
  local copies, waits for them, and re-layouts  9.84 us (3%)
    psum x1, waiting for transfers between devices, shards(): held_total = lax.psum(held_part, 'fsdp')  112 us
    all_gather x1, waiting for transfers between devices, shards(): held_every = lax.all_gather(held_features, 'ex', axis=0, tiled=True)  59.7 us
    all_gather x1, waiting for transfers between devices, shards(): lax.all_gather(adapter_up, 'fsdp', axis=1, tiled=True)  52.5 us
    all_gather x1, waiting for transfers between devices, shards(): lax.all_gather(adapter_down, 'fsdp', axis=0, tiled=True)  22.9 us
    all_gather x1, blocking collectives, shards(): lax.all_gather(width_signs_up, 'fsdp', axis=0, tiled=True)  20.7 us
    all_gather x1, blocking collectives, shards(): lax.all_gather(width_signs_down, 'fsdp', axis=0, tiled=True)  18.8 us
    dot_general x2, matrix products, explicit_terms(): jnp.einsum('esr,esd->erd', hidden, upstream.astype(jnp.float32), precisio...  8.1 us
    unnamed x27, local copies, waits for them, and re-layouts  7.32 us
  transfers between devices with their start and end apart: 4, of which 4 were waited for; matrix products, arithmetic and copies ran while one was open for 7% of the time, Pallas kernels for 0%

commit v1 on v0

v1 whole, which is shorter than its diff:
```python
import functools
import math

import jax
import jax.numpy as jnp
from jax import lax
from jax.experimental import pallas as pl
from jax.experimental.pallas import tpu as pltpu
from jax.sharding import Mesh, PartitionSpec as P

EPSILON = 1e-06
HIGH = lax.Precision.HIGHEST
PLANE = ("c", "y", "x")
EXTRA = 16
LIFT = 14.0
PRODUCTS = 40
COST = 20_000_000_000


def nt(a, b, precision=None):
    return lax.dot_general(
        a, b, (((1,), (1,)), ((), ())), precision=precision, preferred_element_type=jnp.float32
    )


def tn(a, b, precision=None):
    return lax.dot_general(
        a, b, (((0,), (0,)), ((), ())), precision=precision, preferred_element_type=jnp.float32
    )


def nn(a, b, precision=None):
    return lax.dot_general(
        a, b, (((1,), (0,)), ((), ())), precision=precision, preferred_element_type=jnp.float32
    )


def prepare_kernel(
    core_ref, down_ref, up_ref, rank_down_ref, rank_up_ref, wide_up_ref, wide_down_ref,
    xt_ref, gt_ref, xh_ref, gh_ref, block_ref, send_ref, adapter, rank, wide, sems,
):
    first = core_ref[0] == 0
    tokens = xt_ref.shape[0]
    held = xh_ref.shape[0]

    def copies(of_adapter, of_rank, of_wide, of_t, of_h):
        return [
            pltpu.make_async_copy(of_adapter, adapter, sems.at[0]),
            pltpu.make_async_copy(of_rank, rank, sems.at[1]),
            pltpu.make_async_copy(of_wide, wide, sems.at[2]),
            pltpu.make_async_copy(of_t, send_ref.at[pl.ds(0, tokens)], sems.at[3]),
            pltpu.make_async_copy(of_h, send_ref.at[pl.ds(tokens, held)], sems.at[4]),
        ]

    of_g = copies(up_ref, rank_down_ref, wide_up_ref, xt_ref, xh_ref)
    of_x = copies(down_ref, rank_up_ref, wide_down_ref, gt_ref, gh_ref)

    @pl.when(first)
    def _():
        for one in of_g:
            one.start()

    @pl.when(jnp.logical_not(first))
    def _():
        for one in of_x:
            one.start()

    for one in of_g[:3]:
        one.wait()
    rows = adapter.shape[0]
    half = rank.shape[0]
    blank = jnp.zeros(rank.shape, rank.dtype)
    mine = rank[...]
    folded = nt(
        adapter[...],
        jnp.concatenate([jnp.where(first, blank, mine), jnp.where(first, mine, blank)], axis=0),
    )
    signs = wide[...].astype(jnp.float32)
    blank = jnp.zeros_like(signs)
    signs = jnp.concatenate([jnp.where(first, signs, blank), jnp.where(first, blank, signs)], axis=0)
    top = jnp.max(jnp.abs(folded), axis=0, keepdims=True)
    exponent = jnp.floor(jnp.log2(jnp.maximum(top, 2.0**-100)))
    lane = lax.broadcasted_iota(jnp.int32, (1, 2 * half), 1)
    is_folded = (lane >= half) == first
    exponent = jnp.where(is_folded, exponent, LIFT)
    block_ref[pl.ds(0, rows), :] = folded * jnp.exp2(LIFT - exponent) + signs.T
    block_ref[pl.ds(rows, EXTRA), :] = jnp.broadcast_to(exponent, (EXTRA, 2 * half))
    for one in of_g[3:]:
        one.wait()


def decode_kernel(values_ref, factor_ref):
    chunks, tall, both = values_ref.shape
    local = tall - EXTRA
    for f in range(chunks):
        scale = jnp.exp2(values_ref[f, pl.ds(local, 1), :] - LIFT)
        value = values_ref[f, pl.ds(0, local), :] * scale
        high = value.astype(jnp.bfloat16)
        factor_ref[pl.ds(f * local, local), pl.ds(0, both)] = high
        low = value - high.astype(jnp.float32)
        factor_ref[pl.ds(f * local, local), pl.ds(both, both)] = low.astype(jnp.bfloat16)


def product_kernel(
    core_ref, factor_ref, xt_ref, gt_ref, xh_ref, gh_ref, recv_ref,
    own_ref, other_ref, held_ref, rows_ref, sems,
):
    first = core_ref[0] == 0
    tokens, width = xt_ref.shape
    held = xh_ref.shape[0]
    both = own_ref.shape[1]

    def copies(of_t, of_h):
        return [
            pltpu.make_async_copy(of_t, rows_ref.at[pl.ds(0, tokens)], sems.at[0]),
            pltpu.make_async_copy(of_h, rows_ref.at[pl.ds(2 * tokens, held)], sems.at[1]),
        ]

    of_x, of_g = copies(xt_ref, xh_ref), copies(gt_ref, gh_ref)
    of_recv = [
        pltpu.make_async_copy(
            recv_ref.at[pl.ds(0, tokens)], rows_ref.at[pl.ds(tokens, tokens)], sems.at[2]
        ),
        pltpu.make_async_copy(
            recv_ref.at[pl.ds(tokens, held)], rows_ref.at[pl.ds(2 * tokens + held, held)], sems.at[3]
        ),
    ]

    @pl.when(first)
    def _():
        for one in of_g:
            one.start()

    @pl.when(jnp.logical_not(first))
    def _():
        for one in of_x:
            one.start()

    for one in of_recv:
        one.start()
    for one in of_g + of_recv:
        one.wait()
    out = nn(rows_ref[...], factor_ref[...])
    out = out[:, :both] + out[:, both:]
    own_ref[...] = out[:tokens]
    other_ref[...] = out[tokens : 2 * tokens]
    own = out[2 * tokens : 2 * tokens + held]
    other = out[2 * tokens + held :]
    held_ref[pl.ds(0, held), :] = jnp.where(first, own, other)
    held_ref[pl.ds(held, held), :] = jnp.where(first, other, own)


def joined(product, half):
    lane = lax.broadcasted_iota(jnp.int32, (half, 2 * half), 1)
    return jnp.where(lane < half, product[:half], product[half:])


def scale_of(values):
    return lax.rsqrt(jnp.sum(values * values, keepdims=True) * (1.0 / values.size) + EPSILON)


def feature_kernel(core_ref, own_ref, recv_ref, held_ref, features_ref, out_ref, *, share, copies):
    first = core_ref[0] == 0
    own, recv = own_ref[...], recv_ref[...]
    of_g = jnp.where(first, own, recv)
    of_x = jnp.where(first, recv, own)
    product = tn(of_x, of_g, HIGH)
    turned = tn(of_g, of_x, HIGH)
    half = product.shape[0] // 2
    values = joined(product, half)
    scale = scale_of(values)
    features_ref[0] = (product * scale)[:half, :half].astype(jnp.bfloat16)
    features_ref[1] = (turned * scale)[half:, half:].astype(jnp.bfloat16)
    rounded = (values * scale).astype(jnp.bfloat16)
    rows = half // copies
    for i in range(out_ref.shape[0]):
        v, j = divmod(i, copies)
        value = held_ref[pl.ds(v * share, share), :]
        high = value.astype(jnp.bfloat16).astype(jnp.float32)
        pair = jnp.concatenate([high, value - high], axis=0).astype(jnp.bfloat16)
        out_ref[i, pl.ds(0, 2 * share), :] = pair
        out_ref[i, pl.ds(2 * share, rows), :] = rounded[j * rows : (j + 1) * rows]


def normal_kernel(part_ref, tokens_ref, out_ref, held_ref, *, share):
    count = tokens_ref.shape[0] // 2
    both = tokens_ref.shape[2]
    pairs = tokens_ref[:, pl.ds(0, 2 * share), :].astype(jnp.float32)
    tokens = (pairs[:, :share] + pairs[:, share:]).reshape(2 * count * share, both)
    product = tn(tokens[count * share :], tokens[: count * share], HIGH)
    half = both // 2
    values = joined(product, half)
    held_ref[...] = values * scale_of(values)
    rows = out_ref.shape[1]
    start = pl.multiple_of(part_ref[0] * rows, rows)
    own = held_ref[pl.ds(start, rows), :].astype(jnp.bfloat16)
    for i in range(out_ref.shape[0]):
        out_ref[i] = own


def influence_kernel(slot_ref, tokens_ref, held_ref, out_ref, *, share, slots):
    mates, _, both = tokens_ref.shape
    rows = tokens_ref.shape[1] - 2 * share
    train = tokens_ref[:, pl.ds(2 * share, rows), :].reshape(mates * rows, both)
    every = nt(train, held_ref[...])
    n, m = every.shape
    r = lax.broadcasted_iota(jnp.int32, (n, m), 0)
    q = lax.broadcasted_iota(jnp.int32, (n, m), 1)
    every = jnp.where(lax.rem(r, rows) == lax.rem(q, rows), every, 0.0)
    trains = n // rows
    summed = jnp.sum(every.reshape(trains, rows // 8, 8, m), axis=1).reshape(trains * 8, m)
    row = lax.broadcasted_iota(jnp.int32, (m, out_ref.shape[1]), 0)
    col = lax.broadcasted_iota(jnp.int32, (m, out_ref.shape[1]), 1)
    place = jnp.where(col == lax.div(row, rows) * slots + slot_ref[0], 1.0, 0.0)
    out_ref[...] = nn(summed, place, HIGH)


SMEM = pl.BlockSpec(memory_space=pltpu.SMEM)
VMEM = pl.BlockSpec(memory_space=pltpu.VMEM)
HBM = pl.BlockSpec(memory_space=pl.ANY)


def shape(dims, dtype=jnp.float32):
    return jax.ShapeDtypeStruct(dims, dtype)


def params(mib):
    return pltpu.CompilerParams(vmem_limit_bytes=mib << 20)


def shards(
    train_inputs, train_upstream, held_inputs, held_upstream, adapter_down, adapter_up,
    rank_signs_up, rank_signs_down, width_signs_up, width_signs_down, *, sizes,
):
    nz, nc, ny, nx = sizes
    mates = nc * ny * nx
    core = lax.axis_index("c").astype(jnp.int32).reshape(1)
    part = lax.axis_index("x").astype(jnp.int32).reshape(1)
    slot = (lax.axis_index("c") * ny + lax.axis_index("y")).astype(jnp.int32).reshape(1)
    tokens, width = train_inputs.shape[1:]
    groups, share = held_inputs.shape[:2]
    held_rows = groups * share
    local, rank = adapter_down.shape
    half = rank_signs_up.shape[1]
    both = 2 * half
    rows = half // nx
    bf16 = jnp.bfloat16
    tall = local + EXTRA
    every_rows = 2 * (tokens + held_rows)

    sequences = (
        train_inputs.reshape(tokens, width), train_upstream.reshape(tokens, width),
        held_inputs.reshape(held_rows, width), held_upstream.reshape(held_rows, width),
    )
    block, send = pl.pallas_call(
        prepare_kernel,
        out_shape=(shape((tall, both)), shape((tokens + held_rows, width), bf16)),
        in_specs=[SMEM] + [HBM] * 10,
        out_specs=(VMEM, VMEM),
        scratch_shapes=[
            pltpu.VMEM((local, rank), bf16),
            pltpu.VMEM((half, rank), bf16),
            pltpu.VMEM((half, local), bf16),
            pltpu.SemaphoreType.DMA((5,)),
        ],
        compiler_params=params(60),
        name="prepare",
    )(
        core, adapter_down, adapter_up.T, rank_signs_down.T, rank_signs_up.T,
        width_signs_up.T, width_signs_down.T, *sequences,
    )
    blocks = jnp.broadcast_to(block.astype(jnp.float16), (ny * nx, tall, both))
    gathered = lax.all_to_all(blocks, ("y", "x"), 0, 0)
    swap = [(0, 1), (1, 0)]
    recv = lax.ppermute(send, "c", swap)

    factor = pl.pallas_call(
        decode_kernel,
        out_shape=shape((width, 2 * both), bf16),
        in_specs=[VMEM],
        out_specs=VMEM,
        compiler_params=params(16),
        cost_estimate=pl.CostEstimate(flops=COST, bytes_accessed=8 * width * both, transcendentals=0),
        name="decode",
    )(gathered.astype(jnp.float32))
    own, other, held_products = pl.pallas_call(
        product_kernel,
        out_shape=(shape((tokens, both)), shape((tokens, both)), shape((2 * held_rows, both))),
        in_specs=[SMEM, VMEM] + [HBM] * 5,
        out_specs=(VMEM, VMEM, VMEM),
        scratch_shapes=[
            pltpu.VMEM((every_rows, width), bf16),
            pltpu.SemaphoreType.DMA((4,)),
        ],
        compiler_params=params(PRODUCTS),
        name="products",
    )(core, factor, *sequences, recv)
    swapped = lax.ppermute(other, "c", swap)

    features, to_plane = pl.pallas_call(
        functools.partial(feature_kernel, share=share, copies=nx),
        out_shape=(shape((2, half, half), bf16), shape((mates, 2 * share + rows, both), bf16)),
        in_specs=[SMEM, VMEM, VMEM, VMEM],
        out_specs=(VMEM, VMEM),
        compiler_params=params(40),
        name="train_features",
    )(core, own, swapped, held_products)
    in_plane = lax.all_to_all(to_plane, PLANE, 0, 0)

    to_z = pl.pallas_call(
        functools.partial(normal_kernel, share=share),
        out_shape=shape((nz, rows, both), bf16),
        in_specs=[SMEM, VMEM],
        out_specs=VMEM,
        scratch_shapes=[pltpu.VMEM((half, both), jnp.float32)],
        compiler_params=params(16),
        name="held_features",
    )(part, in_plane)
    held_every = lax.all_to_all(to_z, "z", 0, 0)

    partial = pl.pallas_call(
        functools.partial(influence_kernel, share=share, slots=nc * ny),
        out_shape=shape((mates * 8, nz * nc * ny)),
        in_specs=[SMEM, VMEM, VMEM],
        out_specs=VMEM,
        compiler_params=params(16),
        name="partial_influence",
    )(slot, in_plane, held_every.reshape(nz * rows, both))
    back = lax.all_to_all(partial.reshape(mates, 8, nz * nc * ny), PLANE, 0, 0)
    influence = jnp.sum(back, axis=(0, 1)).reshape(1, -1) * (1.0 / math.sqrt(half * both))
    return features.reshape(1, half * both), influence


def solution(mesh):
    ex, fsdp = mesh.devices.shape
    ny = nx = math.isqrt(fsdp)
    sizes = (ex // 2, 2, ny, nx)
    fine = Mesh(mesh.devices.reshape(sizes), ("z", "c", "y", "x"))
    e, f = ("z", "c"), ("y", "x")
    every = ("z", "c", "y", "x")
    placed = (
        P(every, None, None), P(every, None, None), P(e, f, None), P(e, f, None),
        P(f, None), P(None, f), P(), P(), P(f, None), P(f, None),
    )
    return jax.shard_map(
        functools.partial(shards, sizes=sizes),
        mesh=fine,
        in_specs=placed,
        out_specs=(P(every, None), P(every, None)),
        check_vma=False,
    )
```

time: 356 us -> 99.3 us (0.28)
  waiting for transfers between devices: 248 us -> 40.4 us
  starting transfers between devices: 0.16 us -> 44.5 us
  matrix products: 39.8 us -> 0 us
  blocking collectives: 39.5 us -> 0 us
  between operations: 14.8 us -> 0.78 us
  Pallas kernels: 0 us -> 8.17 us
  local copies, waits for them, and re-layouts: 9.84 us -> 3.24 us
    all_gather x3 -> x0, waiting for transfers between devices: 135 us -> none  [the longest x1 59.7 us: shards(): held_every = lax.all_gather(held_features, 'ex', axis=0, tiled=True)]
    psum x1 -> x0, waiting for transfers between devices: 112 us -> none  [shards(): held_total = lax.psum(held_part, 'fsdp')]
    dot_general x17 -> x0, matrix products: 39.8 us -> none  [the longest x2 8.1 us: explicit_terms(): jnp.einsum('esr,esd->erd', hidden, upstream.astype(jnp.float32), precisio...]
    all_to_all x0 -> x4, waiting for transfers between devices: none -> 39.6 us  [the longest x1 12.9 us: shards(): gathered = lax.all_to_all(blocks, ('y', 'x'), 0, 0)]
    all_gather x2 -> x0, blocking collectives: 39.5 us -> none  [the longest x1 20.7 us: shards(): lax.all_gather(width_signs_up, 'fsdp', axis=0, tiled=True)]
    all_to_all x0 -> x4, starting transfers between devices: none -> 33 us  [the longest x1 15.2 us: shards(): held_every = lax.all_to_all(to_z, 'z', 0, 0)]
    ppermute x0 -> x2, starting transfers between devices: none -> 11.5 us  [the longest x1 6.58 us: shards(): swapped = lax.ppermute(other, 'c', swap)]
    pallas_call x0 -> x6, Pallas kernels: none -> 8.17 us  [the longest x1 2.75 us: shards(): pl.pallas_call(prepare_kernel, out_shape=(shape((tall, both)), shape((tok...]
  transfers between devices with their start and end apart: 4 -> 6, of which waited for: 4 -> 5; matrix products, arithmetic and copies ran while one was open for 7% -> 1% of each run, Pallas kernels for 0% -> 1%
where the time goes in v1:
time: 99.3 us; the launch traced here: 98.8 us
  starting transfers between devices  44.5 us (45%)
  waiting for transfers between devices  40.4 us (41%)
  Pallas kernels  8.17 us (8%)
  local copies, waits for them, and re-layouts  3.24 us (3%)
  other arithmetic  1.68 us (2%)
    all_to_all x1, starting transfers between devices, shards(): held_every = lax.all_to_all(to_z, 'z', 0, 0)  15.2 us
    all_to_all x1, waiting for transfers between devices, shards(): gathered = lax.all_to_all(blocks, ('y', 'x'), 0, 0)  12.9 us
    all_to_all x1, waiting for transfers between devices, shards(): held_every = lax.all_to_all(to_z, 'z', 0, 0)  11.6 us
    all_to_all x1, waiting for transfers between devices, shards(): in_plane = lax.all_to_all(to_plane, PLANE, 0, 0)  8.27 us
    all_to_all x1, starting transfers between devices, shards(): gathered = lax.all_to_all(blocks, ('y', 'x'), 0, 0)  7.58 us
    all_to_all x1, waiting for transfers between devices, shards(): back = lax.all_to_all(partial.reshape(mates, 8, nz * nc * ny), PLANE, 0, 0)  6.83 us
    ppermute x1, starting transfers between devices, shards(): swapped = lax.ppermute(other, 'c', swap)  6.58 us
    all_to_all x1, starting transfers between devices, shards(): back = lax.all_to_all(partial.reshape(mates, 8, nz * nc * ny), PLANE, 0, 0)  6.27 us
  transfers between devices with their start and end apart: 6, of which 5 were waited for; matrix products, arithmetic and copies ran while one was open for 1% of the time, Pallas kernels for 1%

profile of v1, /device:TPU:1, one launch (start us, length us, event | category | flops | bytes accessed | tf_op | source)
XLA Modules:
  0.0 98.8 jit_solution(13003248830876585053)
XLA Ops:
  0.6 2.8 %prepare.1 = (f32[336,128]{1,0:T(8,128)}, bf16[160,5120]{1,0:T(8,128)(2,1)}) custom-call(s32[1]{0:T(128)} %bitcast.core_ref, bf16[320,128]{1,0:T(8,128)(2,1)} %down_ref.1, bf16[320,128]{1,0:T(8,128)(2,1)} %bitcast.25, bf16[64,128]{1,0:T(8,128)(2,1)} %bitcast.28, bf16[64,128]{1,0:T(8,128)(2,1)} %bitcast.29, bf16[64,320]{1,0:T(8,128)(2,1)} %bitcast.26, ...), custom_call_target="tpu_custom_call" | custom-call | tf_op jit(solution)/shard_map/prepare/pallas_call | solution.py:255
  3.4 0.9 convert_element_type.6
  4.3 1.3 %broadcast_in_dim.3 = f16[16,336,128]{2,1,0:T(8,128)(2,1)} broadcast(f16[336,128]{1,0:T(8,128)(2,1)S(1)} %convert_element_type.6), dimensions={1,2} | broadcast | bytes 1462272 | tf_op jit(solution)/shard_map/broadcast_in_dim | solution.py:272
  5.6 7.6 %all-to-all-start = ((f16[16,336,128]{2,1,0:T(8,128)(2,1)}), f16[16,336,128]{2,1,0:T(8,128)(2,1)S(1)}, u32[]{:S(2)}, u32[]{:S(2)}) async-start(f16[16,336,128]{2,1,0:T(8,128)(2,1)} %broadcast_in_dim.3), calls=%async_computation | async-start | bytes 2752512 | tf_op jit(solution)/shard_map/all_to_all | solution.py:273
  13.2 4.9 %collective-permute-start = (bf16[160,5120]{1,0:T(8,128)(2,1)}, bf16[160,5120]{1,0:T(8,128)(2,1)S(1)}, u32[]{:S(2)}, u32[]{:S(2)}) collective-permute-start(bf16[160,5120]{1,0:T(8,128)(2,1)} %get-tuple-element.10), channel_id=1, source_target_pairs={{0,16},{16,0},{1,17},{17,1},{2,18},{18,2},{3,19},{19,3},{4,20},{20... | collective-permute-start | bytes 4915208 | tf_op jit(solution)/shard_map/ppermute | solution.py:275
  18.1 12.9 %all-to-all-done = f16[16,336,128]{2,1,0:T(8,128)(2,1)S(1)} async-done(((f16[16,336,128]{2,1,0:T(8,128)(2,1)}), f16[16,336,128]{2,1,0:T(8,128)(2,1)S(1)}, u32[]{:S(2)}, u32[]{:S(2)}) %all-to-all-start) | async-done | bytes 1376288 | tf_op jit(solution)/shard_map/all_to_all | solution.py:273
  31.0 0.2 convert_element_type.7.values_ref
  31.2 0.0 copy-start
  31.2 0.0 copy-start.1
  31.2 0.0 copy-start.2
  31.2 0.0 copy-start.3
  31.2 0.6 decode.1.factor_ref
  31.8 0.0 collective-permute-done.recv_ref
  31.8 0.7 copy-done
  32.5 0.4 copy-done.1
  32.9 0.0 copy-done.2
  32.9 0.1 copy-done.3
  33.0 1.4 %products.1 = (f32[128,128]{1,0:T(8,128)S(1)}, f32[128,128]{1,0:T(8,128)S(1)}, f32[64,128]{1,0:T(8,128)S(1)}) custom-call(s32[1]{0:T(128)} %bitcast.core_ref, bf16[5120,256]{1,0:T(8,128)(2,1)S(1)} %decode.1.factor_ref, bf16[128,5120]{1,0:T(8,128)(2,1)S(1)} %bitcast.17, bf16[128,5120]{1,0:T(8,128)(2,1)S(1)} %bitcast.19, bf16[32,5120]{1,0:T(8,128)(2,1)S(1)} %bitcast.21, ...), custom_call_target="tpu_custom_call" | custom-call | tf_op jit(solution)/shard_map/products/pallas_call | solution.py:286
  34.5 6.6 %collective-permute-start.1 = (f32[128,128]{1,0:T(8,128)S(1)}, f32[128,128]{1,0:T(8,128)S(1)}, u32[]{:S(2)}, u32[]{:S(2)}) collective-permute-start(f32[128,128]{1,0:T(8,128)S(1)} %get-tuple-element.12), channel_id=1, source_target_pairs={{0,16},{16,0},{1,17},{17,1},{2,18},{18,2},{3,19},{19,3},{4,20},{20... | collective-permute-start | bytes 196616 | tf_op jit(solution)/shard_map/ppermute | solution.py:298
  41.1 0.9 collective-permute-done.1.recv_ref
  41.9 1.2 %train_features.1 = (bf16[2,64,64]{2,1,0:T(8,128)(2,1)S(1)}, bf16[32,32,128]{2,1,0:T(8,128)(2,1)}) custom-call(s32[1]{0:T(128)} %bitcast.core_ref, f32[128,128]{1,0:T(8,128)S(1)} %get-tuple-element.11.own_ref, f32[128,128]{1,0:T(8,128)S(1)} %collective-permute-done.1.recv_ref, f32[64,128]{1,0:T(8,128)S(1)} %get-tuple-element.13.held_ref), custom_call_target="tpu_custom_call" | custom-call | tf_op jit(solution)/shard_map/train_features/pallas_call | solution.py:300
  43.1 4.0 %all-to-all-start.1 = ((bf16[32,32,128]{2,1,0:T(8,128)(2,1)}), bf16[32,32,128]{2,1,0:T(8,128)(2,1)S(1)}, u32[]{:S(2)}, u32[]{:S(2)}) async-start(bf16[32,32,128]{2,1,0:T(8,128)(2,1)} %get-tuple-element.15), calls=%async_computation.1 | async-start | bytes 524288 | tf_op jit(solution)/shard_map/all_to_all | solution.py:308
  47.1 8.3 %all-to-all-done.1.tokens_ref = bf16[32,32,128]{2,1,0:T(8,128)(2,1)S(1)} async-done(((bf16[32,32,128]{2,1,0:T(8,128)(2,1)}), bf16[32,32,128]{2,1,0:T(8,128)(2,1)S(1)}, u32[]{:S(2)}, u32[]{:S(2)}) %all-to-all-start.1) | async-done | bytes 262176 | tf_op jit(solution)/shard_map/all_to_all | solution.py:308
  55.4 1.0 %held_features.1 = bf16[16,16,128]{2,1,0:T(8,128)(2,1)} custom-call(s32[1]{0:T(128)} %bitcast.11.part_ref, bf16[32,32,128]{2,1,0:T(8,128)(2,1)S(1)} %all-to-all-done.1.tokens_ref), custom_call_target="tpu_custom_call" | custom-call | tf_op jit(solution)/shard_map/held_features/pallas_call | solution.py:310
  56.4 15.2 %all-to-all-start.2 = ((bf16[16,16,128]{2,1,0:T(8,128)(2,1)}), bf16[16,16,128]{2,1,0:T(8,128)(2,1)S(1)}, u32[]{:S(2)}, u32[]{:S(2)}) async-start(bf16[16,16,128]{2,1,0:T(8,128)(2,1)} %held_features.1), calls=%async_computation.2 | async-start | bytes 131072 | tf_op jit(solution)/shard_map/all_to_all | solution.py:319
  71.6 11.6 %all-to-all-done.2 = bf16[16,16,128]{2,1,0:T(8,128)(2,1)S(1)} async-done(((bf16[16,16,128]{2,1,0:T(8,128)(2,1)}), bf16[16,16,128]{2,1,0:T(8,128)(2,1)S(1)}, u32[]{:S(2)}, u32[]{:S(2)}) %all-to-all-start.2) | async-done | bytes 65568 | tf_op jit(solution)/shard_map/all_to_all | solution.py:319
  83.1 1.3 %partial_influence.1 = f32[256,128]{1,0:T(8,128)} custom-call(s32[1]{0:T(128)} %bitcast.10.slot_ref, bf16[32,32,128]{2,1,0:T(8,128)(2,1)S(1)} %all-to-all-done.1.tokens_ref, bf16[256,128]{1,0:T(8,128)(2,1)S(1)} %bitcast.24), custom_call_target="tpu_custom_call" | custom-call | tf_op jit(solution)/shard_map/partial_influence/pallas_call | solution.py:321
  84.4 6.3 %all-to-all-start.3 = ((f32[32,8,128]{2,1,0:T(8,128)}), f32[32,8,128]{2,1,0:T(8,128)S(1)}, u32[]{:S(2)}, u32[]{:S(2)}) async-start(f32[32,8,128]{2,1,0:T(8,128)} %bitcast.13), calls=%async_computation.3 | async-start | bytes 262144 | tf_op jit(solution)/shard_map/all_to_all | solution.py:329
  90.7 0.7 reshape.50
  91.4 6.8 %all-to-all-done.3 = f32[32,8,128]{2,1,0:T(8,128)S(1)} async-done(((f32[32,8,128]{2,1,0:T(8,128)}), f32[32,8,128]{2,1,0:T(8,128)S(1)}, u32[]{:S(2)}, u32[]{:S(2)}) %all-to-all-start.3) | async-done | bytes 131104 | tf_op jit(solution)/shard_map/all_to_all | solution.py:329
  98.3 0.5 multiply_bitcast_fusion
  (1 shorter events, 0.0 us)
Async XLA Ops:
  5.6 25.4 %all-to-all-start = ((f16[16,336,128]{2,1,0:T(8,128)(2,1)}), f16[16,336,128]{2,1,0:T(8,128)(2,1)S(1)}, u32[]{:S(2)}, u32[]{:S(2)}) async-start(f16[16,336,128]{2,1,0:T(8,128)(2,1)} %broadcast_in_dim.3), calls=%async_computation | async-start | bytes 2752512 | tf_op jit(solution)/shard_map/all_to_all | solution.py:273
  13.2 18.6 %collective-permute-start = (bf16[160,5120]{1,0:T(8,128)(2,1)}, bf16[160,5120]{1,0:T(8,128)(2,1)S(1)}, u32[]{:S(2)}, u32[]{:S(2)}) collective-permute-start(bf16[160,5120]{1,0:T(8,128)(2,1)} %get-tuple-element.10), channel_id=1, source_target_pairs={{0,16},{16,0},{1,17},{17,1},{2,18},{18,2},{3,19},{19,3},{4,20},{20... | collective-permute-start | bytes 4915208 | tf_op jit(solution)/shard_map/ppermute | solution.py:275
  31.2 1.3 %copy-start = (bf16[1,128,5120]{2,1,0:T(8,128)(2,1)S(1)}, bf16[1,128,5120]{2,1,0:T(8,128)(2,1)}, u32[]{:S(2)}) copy-start(bf16[1,128,5120]{2,1,0:T(8,128)(2,1)} %param.10) | copy-start | bytes 3932164
  31.2 1.7 %copy-start.1 = (bf16[1,128,5120]{2,1,0:T(8,128)(2,1)S(1)}, bf16[1,128,5120]{2,1,0:T(8,128)(2,1)}, u32[]{:S(2)}) copy-start(bf16[1,128,5120]{2,1,0:T(8,128)(2,1)} %param.11) | copy-start | bytes 3932164
  31.2 1.7 %copy-start.2 = (bf16[4,8,5120]{2,1,0:T(8,128)(2,1)S(1)}, bf16[4,8,5120]{2,1,0:T(8,128)(2,1)}, u32[]{:S(2)}) copy-start(bf16[4,8,5120]{2,1,0:T(8,128)(2,1)} %param.12) | copy-start | bytes 983044
  31.2 1.8 %copy-start.3 = (bf16[4,8,5120]{2,1,0:T(8,128)(2,1)S(1)}, bf16[4,8,5120]{2,1,0:T(8,128)(2,1)}, u32[]{:S(2)}) copy-start(bf16[4,8,5120]{2,1,0:T(8,128)(2,1)} %param.13) | copy-start | bytes 983044
  34.5 7.5 %collective-permute-start.1 = (f32[128,128]{1,0:T(8,128)S(1)}, f32[128,128]{1,0:T(8,128)S(1)}, u32[]{:S(2)}, u32[]{:S(2)}) collective-permute-start(f32[128,128]{1,0:T(8,128)S(1)} %get-tuple-element.12), channel_id=1, source_target_pairs={{0,16},{16,0},{1,17},{17,1},{2,18},{18,2},{3,19},{19,3},{4,20},{20... | collective-permute-start | bytes 196616 | tf_op jit(solution)/shard_map/ppermute | solution.py:298
  43.1 12.3 %all-to-all-start.1 = ((bf16[32,32,128]{2,1,0:T(8,128)(2,1)}), bf16[32,32,128]{2,1,0:T(8,128)(2,1)S(1)}, u32[]{:S(2)}, u32[]{:S(2)}) async-start(bf16[32,32,128]{2,1,0:T(8,128)(2,1)} %get-tuple-element.15), calls=%async_computation.1 | async-start | bytes 524288 | tf_op jit(solution)/shard_map/all_to_all | solution.py:308
  56.4 26.8 %all-to-all-start.2 = ((bf16[16,16,128]{2,1,0:T(8,128)(2,1)}), bf16[16,16,128]{2,1,0:T(8,128)(2,1)S(1)}, u32[]{:S(2)}, u32[]{:S(2)}) async-start(bf16[16,16,128]{2,1,0:T(8,128)(2,1)} %held_features.1), calls=%async_computation.2 | async-start | bytes 131072 | tf_op jit(solution)/shard_map/all_to_all | solution.py:319
  84.4 13.8 %all-to-all-start.3 = ((f32[32,8,128]{2,1,0:T(8,128)}), f32[32,8,128]{2,1,0:T(8,128)S(1)}, u32[]{:S(2)}, u32[]{:S(2)}) async-start(f32[32,8,128]{2,1,0:T(8,128)} %bitcast.13), calls=%async_computation.3 | async-start | bytes 262144 | tf_op jit(solution)/shard_map/all_to_all | solution.py:329

commit v2 on v1

--- a/solution.py
+++ b/solution.py
@@ -11,9 +11,8 @@
 EPSILON = 1e-06
 HIGH = lax.Precision.HIGHEST
 PLANE = ("c", "y", "x")
-EXTRA = 16
+EXTRA = 8
 LIFT = 14.0
-PRODUCTS = 40
 COST = 20_000_000_000
 
 
@@ -37,23 +36,19 @@
 
 def prepare_kernel(
     core_ref, down_ref, up_ref, rank_down_ref, rank_up_ref, wide_up_ref, wide_down_ref,
-    xt_ref, gt_ref, xh_ref, gh_ref, block_ref, send_ref, adapter, rank, wide, sems,
+    block_ref, adapter, rank, wide, sems,
 ):
     first = core_ref[0] == 0
-    tokens = xt_ref.shape[0]
-    held = xh_ref.shape[0]
-
-    def copies(of_adapter, of_rank, of_wide, of_t, of_h):
+
+    def copies(of_adapter, of_rank, of_wide):
         return [
             pltpu.make_async_copy(of_adapter, adapter, sems.at[0]),
             pltpu.make_async_copy(of_rank, rank, sems.at[1]),
             pltpu.make_async_copy(of_wide, wide, sems.at[2]),
-            pltpu.make_async_copy(of_t, send_ref.at[pl.ds(0, tokens)], sems.at[3]),
-            pltpu.make_async_copy(of_h, send_ref.at[pl.ds(tokens, held)], sems.at[4]),
         ]
 
-    of_g = copies(up_ref, rank_down_ref, wide_up_ref, xt_ref, xh_ref)
-    of_x = copies(down_ref, rank_up_ref, wide_down_ref, gt_ref, gh_ref)
+    of_g = copies(up_ref, rank_down_ref, wide_up_ref)
+    of_x = copies(down_ref, rank_up_ref, wide_down_ref)
 
     @pl.when(first)
     def _():
@@ -65,7 +60,7 @@
         for one in of_x:
             one.start()
 
-    for one in of_g[:3]:
+    for one in of_g:
         one.wait()
     rows = adapter.shape[0]
     half = rank.shape[0]
@@ -85,7 +80,35 @@
     exponent = jnp.where(is_folded, exponent, LIFT)
     block_ref[pl.ds(0, rows), :] = folded * jnp.exp2(LIFT - exponent) + signs.T
     block_ref[pl.ds(rows, EXTRA), :] = jnp.broadcast_to(exponent, (EXTRA, 2 * half))
-    for one in of_g[3:]:
+
+
+def pick_kernel(core_ref, xt_ref, gt_ref, xh_ref, gh_ref, keep_ref, send_ref, sems):
+    first = core_ref[0] == 0
+    tokens = xt_ref.shape[0]
+    held = xh_ref.shape[0]
+
+    def copies(own_t, own_h, other_t, other_h):
+        return [
+            pltpu.make_async_copy(other_t, send_ref.at[pl.ds(0, tokens)], sems.at[0]),
+            pltpu.make_async_copy(other_h, send_ref.at[pl.ds(tokens, held)], sems.at[1]),
+            pltpu.make_async_copy(own_t, keep_ref.at[pl.ds(0, tokens)], sems.at[2]),
+            pltpu.make_async_copy(own_h, keep_ref.at[pl.ds(tokens, held)], sems.at[3]),
+        ]
+
+    of_g = copies(gt_ref, gh_ref, xt_ref, xh_ref)
+    of_x = copies(xt_ref, xh_ref, gt_ref, gh_ref)
+
+    @pl.when(first)
+    def _():
+        for one in of_g:
+            one.start()
+
+    @pl.when(jnp.logical_not(first))
+    def _():
+        for one in of_x:
+            one.start()
+
+    for one in of_g:
         one.wait()
 
 
@@ -101,53 +124,13 @@
         factor_ref[pl.ds(f * local, local), pl.ds(both, both)] = low.astype(jnp.bfloat16)
 
 
-def product_kernel(
-    core_ref, factor_ref, xt_ref, gt_ref, xh_ref, gh_ref, recv_ref,
-    own_ref, other_ref, held_ref, rows_ref, sems,
-):
-    first = core_ref[0] == 0
-    tokens, width = xt_ref.shape
-    held = xh_ref.shape[0]
-    both = own_ref.shape[1]
-
-    def copies(of_t, of_h):
-        return [
-            pltpu.make_async_copy(of_t, rows_ref.at[pl.ds(0, tokens)], sems.at[0]),
-            pltpu.make_async_copy(of_h, rows_ref.at[pl.ds(2 * tokens, held)], sems.at[1]),
-        ]
-
-    of_x, of_g = copies(xt_ref, xh_ref), copies(gt_ref, gh_ref)
-    of_recv = [
-        pltpu.make_async_copy(
-            recv_ref.at[pl.ds(0, tokens)], rows_ref.at[pl.ds(tokens, tokens)], sems.at[2]
-        ),
-        pltpu.make_async_copy(
-            recv_ref.at[pl.ds(tokens, held)], rows_ref.at[pl.ds(2 * tokens + held, held)], sems.at[3]
-        ),
-    ]
-
-    @pl.when(first)
-    def _():
-        for one in of_g:
-            one.start()
-
-    @pl.when(jnp.logical_not(first))
-    def _():
-        for one in of_x:
-            one.start()
-
-    for one in of_recv:
-        one.start()
-    for one in of_g + of_recv:
-        one.wait()
-    out = nn(rows_ref[...], factor_ref[...])
-    out = out[:, :both] + out[:, both:]
-    own_ref[...] = out[:tokens]
-    other_ref[...] = out[tokens : 2 * tokens]
-    own = out[2 * tokens : 2 * tokens + held]
-    other = out[2 * tokens + held :]
-    held_ref[pl.ds(0, held), :] = jnp.where(first, own, other)
-    held_ref[pl.ds(held, held), :] = jnp.where(first, other, own)
+def product_kernel(factor_ref, rows_ref, *refs):
+    train_ref, held_ref = refs[-2:]
+    tokens, both = train_ref.shape
+    value = nn(rows_ref[...], factor_ref[...])
+    value = value[:, :both] + value[:, both:]
+    train_ref[...] = value[:tokens]
+    held_ref[...] = value[tokens:]
 
 
 def joined(product, half):
@@ -159,27 +142,44 @@
     return lax.rsqrt(jnp.sum(values * values, keepdims=True) * (1.0 / values.size) + EPSILON)
 
 
-def feature_kernel(core_ref, own_ref, recv_ref, held_ref, features_ref, out_ref, *, share, copies):
+def kinds(core_ref, own_ref, pair_ref):
     first = core_ref[0] == 0
-    own, recv = own_ref[...], recv_ref[...]
-    of_g = jnp.where(first, own, recv)
-    of_x = jnp.where(first, recv, own)
+    own = own_ref[...]
+    return jnp.where(first, own, pair_ref[0]), jnp.where(first, pair_ref[1], own)
+
+
+def spread_kernel(
+    core_ref, own_ref, pair_ref, held_own_ref, held_other_ref, out_ref, scale_ref, *, share, copies
+):
+    of_g, of_x = kinds(core_ref, own_ref, pair_ref)
     product = tn(of_x, of_g, HIGH)
-    turned = tn(of_g, of_x, HIGH)
     half = product.shape[0] // 2
     values = joined(product, half)
     scale = scale_of(values)
-    features_ref[0] = (product * scale)[:half, :half].astype(jnp.bfloat16)
-    features_ref[1] = (turned * scale)[half:, half:].astype(jnp.bfloat16)
+    scale_ref[...] = jnp.broadcast_to(scale, scale_ref.shape)
     rounded = (values * scale).astype(jnp.bfloat16)
     rows = half // copies
-    for i in range(out_ref.shape[0]):
-        v, j = divmod(i, copies)
-        value = held_ref[pl.ds(v * share, share), :]
-        high = value.astype(jnp.bfloat16).astype(jnp.float32)
-        pair = jnp.concatenate([high, value - high], axis=0).astype(jnp.bfloat16)
-        out_ref[i, pl.ds(0, 2 * share), :] = pair
-        out_ref[i, pl.ds(2 * share, rows), :] = rounded[j * rows : (j + 1) * rows]
+    groups = out_ref.shape[0] // (2 * copies)
+    first = core_ref[0] == 0
+    own, other = held_own_ref[...], held_other_ref[...]
+    for c, held in enumerate((jnp.where(first, own, other), jnp.where(first, other, own))):
+        high = held.astype(jnp.bfloat16).astype(jnp.float32)
+        low = held - high
+        for v in range(groups):
+            part = slice(v * share, (v + 1) * share)
+            pair = jnp.concatenate([high[part], low[part]], axis=0).astype(jnp.bfloat16)
+            for j in range(copies):
+                i = (c * groups + v) * copies + j
+                out_ref[i, pl.ds(0, 2 * share), :] = pair
+                out_ref[i, pl.ds(2 * share, rows), :] = rounded[j * rows : (j + 1) * rows]
+
+
+def feature_kernel(core_ref, own_ref, pair_ref, scale_ref, features_ref):
+    of_g, of_x = kinds(core_ref, own_ref, pair_ref)
+    half = features_ref.shape[1]
+    scale = scale_ref[pl.ds(0, 1), :]
+    features_ref[0] = (tn(of_x, of_g, HIGH) * scale)[:half, :half].astype(jnp.bfloat16)
+    features_ref[1] = (tn(of_g, of_x, HIGH) * scale)[half:, half:].astype(jnp.bfloat16)
 
 
 def normal_kernel(part_ref, tokens_ref, out_ref, held_ref, *, share):
@@ -246,31 +246,39 @@
     rows = half // nx
     bf16 = jnp.bfloat16
     tall = local + EXTRA
-    every_rows = 2 * (tokens + held_rows)
 
     sequences = (
         train_inputs.reshape(tokens, width), train_upstream.reshape(tokens, width),
         held_inputs.reshape(held_rows, width), held_upstream.reshape(held_rows, width),
     )
-    block, send = pl.pallas_call(
+    block = pl.pallas_call(
         prepare_kernel,
-        out_shape=(shape((tall, both)), shape((tokens + held_rows, width), bf16)),
-        in_specs=[SMEM] + [HBM] * 10,
-        out_specs=(VMEM, VMEM),
+        out_shape=shape((tall, both)),
+        in_specs=[SMEM] + [HBM] * 6,
+        out_specs=VMEM,
         scratch_shapes=[
             pltpu.VMEM((local, rank), bf16),
             pltpu.VMEM((half, rank), bf16),
             pltpu.VMEM((half, local), bf16),
-            pltpu.SemaphoreType.DMA((5,)),
+            pltpu.SemaphoreType.DMA((3,)),
         ],
         compiler_params=params(60),
         name="prepare",
     )(
         core, adapter_down, adapter_up.T, rank_signs_down.T, rank_signs_up.T,
-        width_signs_up.T, width_signs_down.T, *sequences,
+        width_signs_up.T, width_signs_down.T,
     )
     blocks = jnp.broadcast_to(block.astype(jnp.float16), (ny * nx, tall, both))
     gathered = lax.all_to_all(blocks, ("y", "x"), 0, 0)
+    keep, send = pl.pallas_call(
+        pick_kernel,
+        out_shape=(shape((tokens + held_rows, width), bf16),) * 2,
+        in_specs=[SMEM] + [HBM] * 4,
+        out_specs=(VMEM, VMEM),
+        scratch_shapes=[pltpu.SemaphoreType.DMA((4,))],
+        compiler_params=params(60),
+        name="pick",
+    )(core, *sequences)
     swap = [(0, 1), (1, 0)]
     recv = lax.ppermute(send, "c", swap)
 
@@ -283,28 +291,36 @@
         cost_estimate=pl.CostEstimate(flops=COST, bytes_accessed=8 * width * both, transcendentals=0),
         name="decode",
     )(gathered.astype(jnp.float32))
-    own, other, held_products = pl.pallas_call(
-        product_kernel,
-        out_shape=(shape((tokens, both)), shape((tokens, both)), shape((2 * held_rows, both))),
-        in_specs=[SMEM, VMEM] + [HBM] * 5,
-        out_specs=(VMEM, VMEM, VMEM),
-        scratch_shapes=[
-            pltpu.VMEM((every_rows, width), bf16),
-            pltpu.SemaphoreType.DMA((4,)),
-        ],
-        compiler_params=params(PRODUCTS),
-        name="products",
-    )(core, factor, *sequences, recv)
-    swapped = lax.ppermute(other, "c", swap)
-
-    features, to_plane = pl.pallas_call(
-        functools.partial(feature_kernel, share=share, copies=nx),
-        out_shape=(shape((2, half, half), bf16), shape((mates, 2 * share + rows, both), bf16)),
-        in_specs=[SMEM, VMEM, VMEM, VMEM],
+    def products(*operands):
+        return pl.pallas_call(
+            product_kernel,
+            out_shape=(shape((tokens, both)), shape((held_rows, both))),
+            in_specs=[VMEM] * len(operands),
+            out_specs=(VMEM, VMEM),
+            compiler_params=params(16),
+            name="products",
+        )(*operands)
+
+    other, held_other = products(factor, recv)
+    own, held_own = products(factor, keep, held_other)
+    pair = lax.all_gather(other, "c")
+
+    to_plane, scale = pl.pallas_call(
+        functools.partial(spread_kernel, share=share, copies=nx),
+        out_shape=(shape((mates, 2 * share + rows, both), bf16), shape((8, both))),
+        in_specs=[SMEM] + [VMEM] * 4,
         out_specs=(VMEM, VMEM),
         compiler_params=params(40),
+        name="spread",
+    )(core, own, pair, held_own, held_other)
+    features = pl.pallas_call(
+        feature_kernel,
+        out_shape=shape((2, half, half), bf16),
+        in_specs=[SMEM] + [VMEM] * 3,
+        out_specs=VMEM,
+        compiler_params=params(16),
         name="train_features",
-    )(core, own, swapped, held_products)
+    )(core, own, pair, scale)
     in_plane = lax.all_to_all(to_plane, PLANE, 0, 0)
 
     to_z = pl.pallas_call(

time: 99.3 us -> 95 us (0.957)
  starting transfers between devices: 44.5 us -> 37.8 us
  blocking collectives: 0 us -> 6.04 us
  waiting for transfers between devices: 40.4 us -> 35.4 us
  Pallas kernels: 8.17 us -> 10.9 us
  local copies, waits for them, and re-layouts: 3.24 us -> 1.98 us
    ppermute x1 -> x0, starting transfers between devices: 6.58 us -> none  [shards(): swapped = lax.ppermute(other, 'c', swap)]
    all_gather x0 -> x1, blocking collectives: none -> 6.04 us  [shards(): pair = lax.all_gather(other, 'c')]
    all_to_all x1, waiting for transfers between devices: 12.9 us -> 9.07 us  [shards(): gathered = lax.all_to_all(blocks, ('y', 'x'), 0, 0)]
    pallas_call x3 -> x6, Pallas kernels: 5.34 us -> 8.08 us  [the longest x1 3.58 us: shards(): pl.pallas_call(pick_kernel, out_shape=(shape((tokens + held_rows, width),...]
    unnamed x8 -> x2, local copies, waits for them, and re-layouts: 1.25 us -> 0.01 us
  transfers between devices with their start and end apart: 6 -> 5, of which waited for: 5 -> 4; matrix products, arithmetic and copies ran while one was open for 1% -> 1% of each run, Pallas kernels for 1% -> 5%
where the time goes in v2:
time: 95 us; the launch traced here: 94.5 us
  starting transfers between devices  37.8 us (40%)
  waiting for transfers between devices  35.4 us (37%)
  Pallas kernels  10.9 us (11%)
  blocking collectives  6.04 us (6%)
  local copies, waits for them, and re-layouts  1.98 us (2%)
  other arithmetic  1.67 us (2%)
    all_to_all x1, starting transfers between devices, shards(): held_every = lax.all_to_all(to_z, 'z', 0, 0)  15.1 us
    all_to_all x1, waiting for transfers between devices, shards(): held_every = lax.all_to_all(to_z, 'z', 0, 0)  11.6 us
    all_to_all x1, waiting for transfers between devices, shards(): gathered = lax.all_to_all(blocks, ('y', 'x'), 0, 0)  9.07 us
    all_to_all x1, waiting for transfers between devices, shards(): in_plane = lax.all_to_all(to_plane, PLANE, 0, 0)  8.27 us
    all_to_all x1, starting transfers between devices, shards(): gathered = lax.all_to_all(blocks, ('y', 'x'), 0, 0)  7.58 us
    all_to_all x1, waiting for transfers between devices, shards(): back = lax.all_to_all(partial.reshape(mates, 8, nz * nc * ny), PLANE, 0, 0)  6.43 us
    all_to_all x1, starting transfers between devices, shards(): back = lax.all_to_all(partial.reshape(mates, 8, nz * nc * ny), PLANE, 0, 0)  6.26 us
    all_gather x1, blocking collectives, shards(): pair = lax.all_gather(other, 'c')  6.04 us
  transfers between devices with their start and end apart: 5, of which 4 were waited for; matrix products, arithmetic and copies ran while one was open for 1% of the time, Pallas kernels for 5%

profile of v2, /device:TPU:1, one launch (start us, length us, event | category | flops | bytes accessed | tf_op | source)
XLA Modules:
  0.0 94.5 jit_solution(12027494475291970648)
XLA Ops:
  0.6 1.8 %prepare.1 = f32[328,128]{1,0:T(8,128)} custom-call(s32[1]{0:T(128)} %bitcast.core_ref, bf16[320,128]{1,0:T(8,128)(2,1)} %down_ref.1, bf16[320,128]{1,0:T(8,128)(2,1)} %bitcast.24, bf16[64,128]{1,0:T(8,128)(2,1)} %bitcast.27, bf16[64,128]{1,0:T(8,128)(2,1)} %bitcast.28, bf16[64,320]{1,0:T(8,128)(2,1)} %bitcast.25, bf16[64,320]{1,0:T(8,128)(2,1)} %bitcast.26), custom_call_target="tpu_custom_call" | custom-call | tf_op jit(solution)/shard_map/prepare/pallas_call | solution.py:254
  2.5 0.9 convert_element_type.6
  3.4 1.3 %broadcast_in_dim.3 = f16[16,328,128]{2,1,0:T(8,128)(2,1)} broadcast(f16[328,128]{1,0:T(8,128)(2,1)S(1)} %convert_element_type.6), dimensions={1,2} | broadcast | bytes 1427456 | tf_op jit(solution)/shard_map/broadcast_in_dim | solution.py:271
  4.7 7.6 %all-to-all-start = ((f16[16,328,128]{2,1,0:T(8,128)(2,1)}), f16[16,328,128]{2,1,0:T(8,128)(2,1)S(1)}, u32[]{:S(2)}, u32[]{:S(2)}) async-start(f16[16,328,128]{2,1,0:T(8,128)(2,1)} %broadcast_in_dim.3), calls=%async_computation | async-start | bytes 2686976 | tf_op jit(solution)/shard_map/all_to_all | solution.py:272
  12.2 3.6 %pick.1 = (bf16[160,5120]{1,0:T(8,128)(2,1)}, bf16[160,5120]{1,0:T(8,128)(2,1)}) custom-call(s32[1]{0:T(128)} %bitcast.core_ref, bf16[128,5120]{1,0:T(8,128)(2,1)} %bitcast.20, bf16[128,5120]{1,0:T(8,128)(2,1)} %bitcast.21, bf16[32,5120]{1,0:T(8,128)(2,1)} %bitcast.22, bf16[32,5120]{1,0:T(8,128)(2,1)} %bitcast.23), custom_call_target="tpu_custom_call" | custom-call | tf_op jit(solution)/shard_map/pick/pallas_call | solution.py:273
  15.8 4.9 %collective-permute-start = (bf16[160,5120]{1,0:T(8,128)(2,1)}, bf16[160,5120]{1,0:T(8,128)(2,1)S(1)}, u32[]{:S(2)}, u32[]{:S(2)}) collective-permute-start(bf16[160,5120]{1,0:T(8,128)(2,1)} %get-tuple-element.11), channel_id=1, source_target_pairs={{0,16},{16,0},{1,17},{17,1},{2,18},{18,2},{3,19},{19,3},{4,20},{20... | collective-permute-start | bytes 4915208 | tf_op jit(solution)/shard_map/ppermute | solution.py:283
  20.7 9.1 %all-to-all-done = f16[16,328,128]{2,1,0:T(8,128)(2,1)S(1)} async-done(((f16[16,328,128]{2,1,0:T(8,128)(2,1)}), f16[16,328,128]{2,1,0:T(8,128)(2,1)S(1)}, u32[]{:S(2)}, u32[]{:S(2)}) %all-to-all-start) | async-done | bytes 1343520 | tf_op jit(solution)/shard_map/all_to_all | solution.py:272
  29.8 0.2 convert_element_type.7.values_ref
  30.0 0.6 decode.1.factor_ref
  30.6 0.0 copy-start
  30.6 0.0 collective-permute-done.rows_ref
  30.6 0.6 products.2
  31.2 6.0 %all-gather = f32[256,128]{1,0:T(8,128)S(1)} all-gather(f32[128,128]{1,0:T(8,128)S(1)} %get-tuple-element.14), channel_id=2, replica_groups=mesh['z'=16,'c'=2,'y'=4,'x'=4] {'c'}, dimensions={0}, use_global_device_ids=true | all-gather | bytes 196608 | tf_op jit(solution)/shard_map/all_gather | solution.py:306
  37.2 0.0 copy-done
  37.2 0.6 products.3
  37.8 1.1 %spread.1 = (bf16[32,32,128]{2,1,0:T(8,128)(2,1)}, f32[8,128]{1,0:T(8,128)S(1)}) custom-call(s32[1]{0:T(128)} %bitcast.core_ref, f32[128,128]{1,0:T(8,128)S(1)} %get-tuple-element.13.own_ref, f32[2,128,128]{2,1,0:T(8,128)S(1)} %bitcast.17, f32[32,128]{1,0:T(8,128)S(1)} %get-tuple-element.15.held_own_ref, f32[32,128]{1,0:T(8,128)S(1)} %get-tuple-element.12.refs_0_.held_other_ref), custom_call_target="tpu_custom_call" | custom-call | tf_op jit(solution)/shard_map/spread/pallas_call | solution.py:308
  38.9 4.0 %all-to-all-start.1 = ((bf16[32,32,128]{2,1,0:T(8,128)(2,1)}), bf16[32,32,128]{2,1,0:T(8,128)(2,1)S(1)}, u32[]{:S(2)}, u32[]{:S(2)}) async-start(bf16[32,32,128]{2,1,0:T(8,128)(2,1)} %get-tuple-element.17), calls=%async_computation.1 | async-start | bytes 524288 | tf_op jit(solution)/shard_map/all_to_all | solution.py:324
  42.9 8.3 %all-to-all-done.1.tokens_ref = bf16[32,32,128]{2,1,0:T(8,128)(2,1)S(1)} async-done(((bf16[32,32,128]{2,1,0:T(8,128)(2,1)}), bf16[32,32,128]{2,1,0:T(8,128)(2,1)S(1)}, u32[]{:S(2)}, u32[]{:S(2)}) %all-to-all-start.1) | async-done | bytes 262176 | tf_op jit(solution)/shard_map/all_to_all | solution.py:324
  51.2 1.0 %held_features.1 = bf16[16,16,128]{2,1,0:T(8,128)(2,1)} custom-call(s32[1]{0:T(128)} %bitcast.12.part_ref, bf16[32,32,128]{2,1,0:T(8,128)(2,1)S(1)} %all-to-all-done.1.tokens_ref), custom_call_target="tpu_custom_call" | custom-call | tf_op jit(solution)/shard_map/held_features/pallas_call | solution.py:326
  52.2 15.1 %all-to-all-start.2 = ((bf16[16,16,128]{2,1,0:T(8,128)(2,1)}), bf16[16,16,128]{2,1,0:T(8,128)(2,1)S(1)}, u32[]{:S(2)}, u32[]{:S(2)}) async-start(bf16[16,16,128]{2,1,0:T(8,128)(2,1)} %held_features.1), calls=%async_computation.2 | async-start | bytes 131072 | tf_op jit(solution)/shard_map/all_to_all | solution.py:335
  67.3 11.6 %all-to-all-done.2 = bf16[16,16,128]{2,1,0:T(8,128)(2,1)S(1)} async-done(((bf16[16,16,128]{2,1,0:T(8,128)(2,1)}), bf16[16,16,128]{2,1,0:T(8,128)(2,1)S(1)}, u32[]{:S(2)}, u32[]{:S(2)}) %all-to-all-start.2) | async-done | bytes 65568 | tf_op jit(solution)/shard_map/all_to_all | solution.py:335
  78.9 1.2 %partial_influence.1 = f32[256,128]{1,0:T(8,128)} custom-call(s32[1]{0:T(128)} %bitcast.11.slot_ref, bf16[32,32,128]{2,1,0:T(8,128)(2,1)S(1)} %all-to-all-done.1.tokens_ref, bf16[256,128]{1,0:T(8,128)(2,1)S(1)} %bitcast.19), custom_call_target="tpu_custom_call" | custom-call | tf_op jit(solution)/shard_map/partial_influence/pallas_call | solution.py:337
  80.1 6.3 %all-to-all-start.3 = ((f32[32,8,128]{2,1,0:T(8,128)}), f32[32,8,128]{2,1,0:T(8,128)S(1)}, u32[]{:S(2)}, u32[]{:S(2)}) async-start(f32[32,8,128]{2,1,0:T(8,128)} %bitcast.14), calls=%async_computation.3 | async-start | bytes 262144 | tf_op jit(solution)/shard_map/all_to_all | solution.py:345
  86.4 0.4 train_features.1
  86.8 0.7 reshape.50
  87.5 6.4 %all-to-all-done.3 = f32[32,8,128]{2,1,0:T(8,128)S(1)} async-done(((f32[32,8,128]{2,1,0:T(8,128)}), f32[32,8,128]{2,1,0:T(8,128)S(1)}, u32[]{:S(2)}, u32[]{:S(2)}) %all-to-all-start.3) | async-done | bytes 131104 | tf_op jit(solution)/shard_map/all_to_all | solution.py:345
  94.0 0.5 multiply_bitcast_fusion
  (1 shorter events, 0.0 us)
Async XLA Ops:
  4.7 25.2 %all-to-all-start = ((f16[16,328,128]{2,1,0:T(8,128)(2,1)}), f16[16,328,128]{2,1,0:T(8,128)(2,1)S(1)}, u32[]{:S(2)}, u32[]{:S(2)}) async-start(f16[16,328,128]{2,1,0:T(8,128)(2,1)} %broadcast_in_dim.3), calls=%async_computation | async-start | bytes 2686976 | tf_op jit(solution)/shard_map/all_to_all | solution.py:272
  15.8 14.7 %collective-permute-start = (bf16[160,5120]{1,0:T(8,128)(2,1)}, bf16[160,5120]{1,0:T(8,128)(2,1)S(1)}, u32[]{:S(2)}, u32[]{:S(2)}) collective-permute-start(bf16[160,5120]{1,0:T(8,128)(2,1)} %get-tuple-element.11), channel_id=1, source_target_pairs={{0,16},{16,0},{1,17},{17,1},{2,18},{18,2},{3,19},{19,3},{4,20},{20... | collective-permute-start | bytes 4915208 | tf_op jit(solution)/shard_map/ppermute | solution.py:283
  30.6 6.7 %copy-start = (bf16[160,5120]{1,0:T(8,128)(2,1)S(1)}, bf16[160,5120]{1,0:T(8,128)(2,1)}, u32[]{:S(2)}) copy-start(bf16[160,5120]{1,0:T(8,128)(2,1)} %get-tuple-element.10.rows_ref) | copy-start | bytes 4915204
  38.9 12.3 %all-to-all-start.1 = ((bf16[32,32,128]{2,1,0:T(8,128)(2,1)}), bf16[32,32,128]{2,1,0:T(8,128)(2,1)S(1)}, u32[]{:S(2)}, u32[]{:S(2)}) async-start(bf16[32,32,128]{2,1,0:T(8,128)(2,1)} %get-tuple-element.17), calls=%async_computation.1 | async-start | bytes 524288 | tf_op jit(solution)/shard_map/all_to_all | solution.py:324
  52.2 26.7 %all-to-all-start.2 = ((bf16[16,16,128]{2,1,0:T(8,128)(2,1)}), bf16[16,16,128]{2,1,0:T(8,128)(2,1)S(1)}, u32[]{:S(2)}, u32[]{:S(2)}) async-start(bf16[16,16,128]{2,1,0:T(8,128)(2,1)} %held_features.1), calls=%async_computation.2 | async-start | bytes 131072 | tf_op jit(solution)/shard_map/all_to_all | solution.py:335
  80.1 13.8 %all-to-all-start.3 = ((f32[32,8,128]{2,1,0:T(8,128)}), f32[32,8,128]{2,1,0:T(8,128)S(1)}, u32[]{:S(2)}, u32[]{:S(2)}) async-start(f32[32,8,128]{2,1,0:T(8,128)} %bitcast.14), calls=%async_computation.3 | async-start | bytes 262144 | tf_op jit(solution)/shard_map/all_to_all | solution.py:345

commit v3 on v2

--- a/solution.py
+++ b/solution.py
@@ -10,7 +10,7 @@
 
 EPSILON = 1e-06
 HIGH = lax.Precision.HIGHEST
-PLANE = ("c", "y", "x")
+PLANE = ("y", "x", "c")
 EXTRA = 8
 LIFT = 14.0
 COST = 20_000_000_000
@@ -35,10 +35,10 @@
 
 
 def prepare_kernel(
-    core_ref, down_ref, up_ref, rank_down_ref, rank_up_ref, wide_up_ref, wide_down_ref,
+    down_ref, up_ref, rank_down_ref, rank_up_ref, wide_up_ref, wide_down_ref,
     block_ref, adapter, rank, wide, sems,
 ):
-    first = core_ref[0] == 0
+    first = lax.axis_index("c") == 0
 
     def copies(of_adapter, of_rank, of_wide):
         return [
@@ -169,7 +169,7 @@
             part = slice(v * share, (v + 1) * share)
             pair = jnp.concatenate([high[part], low[part]], axis=0).astype(jnp.bfloat16)
             for j in range(copies):
-                i = (c * groups + v) * copies + j
+                i = (v * copies + j) * 2 + c
                 out_ref[i, pl.ds(0, 2 * share), :] = pair
                 out_ref[i, pl.ds(2 * share, rows), :] = rounded[j * rows : (j + 1) * rows]
 
@@ -186,8 +186,10 @@
     count = tokens_ref.shape[0] // 2
     both = tokens_ref.shape[2]
     pairs = tokens_ref[:, pl.ds(0, 2 * share), :].astype(jnp.float32)
-    tokens = (pairs[:, :share] + pairs[:, share:]).reshape(2 * count * share, both)
-    product = tn(tokens[count * share :], tokens[: count * share], HIGH)
+    tokens = (pairs[:, :share] + pairs[:, share:]).reshape(count, 2, share, both)
+    of_g = tokens[:, 0].reshape(count * share, both)
+    of_x = tokens[:, 1].reshape(count * share, both)
+    product = tn(of_x, of_g, HIGH)
     half = both // 2
     values = joined(product, half)
     held_ref[...] = values * scale_of(values)
@@ -208,11 +210,13 @@
     q = lax.broadcasted_iota(jnp.int32, (n, m), 1)
     every = jnp.where(lax.rem(r, rows) == lax.rem(q, rows), every, 0.0)
     trains = n // rows
-    summed = jnp.sum(every.reshape(trains, rows // 8, 8, m), axis=1).reshape(trains * 8, m)
-    row = lax.broadcasted_iota(jnp.int32, (m, out_ref.shape[1]), 0)
-    col = lax.broadcasted_iota(jnp.int32, (m, out_ref.shape[1]), 1)
+    summed = jnp.sum(every.reshape(trains, rows, m), axis=1)
+    row = lax.broadcasted_iota(jnp.int32, (m, out_ref.shape[2]), 0)
+    col = lax.broadcasted_iota(jnp.int32, (m, out_ref.shape[2]), 1)
     place = jnp.where(col == lax.div(row, rows) * slots + slot_ref[0], 1.0, 0.0)
-    out_ref[...] = nn(summed, place, HIGH)
+    placed = nn(summed, place, HIGH)
+    for i in range(trains):
+        out_ref[i] = placed[i : i + 1]
 
 
 SMEM = pl.BlockSpec(memory_space=pltpu.SMEM)
@@ -251,10 +255,11 @@
         train_inputs.reshape(tokens, width), train_upstream.reshape(tokens, width),
         held_inputs.reshape(held_rows, width), held_upstream.reshape(held_rows, width),
     )
+    pin = lambda v: pltpu.with_memory_space_constraint(v, pltpu.HBM)
     block = pl.pallas_call(
         prepare_kernel,
         out_shape=shape((tall, both)),
-        in_specs=[SMEM] + [HBM] * 6,
+        in_specs=[HBM] * 6,
         out_specs=VMEM,
         scratch_shapes=[
             pltpu.VMEM((local, rank), bf16),
@@ -262,11 +267,13 @@
             pltpu.VMEM((half, local), bf16),
             pltpu.SemaphoreType.DMA((3,)),
         ],
-        compiler_params=params(60),
+        compiler_params=params(16),
         name="prepare",
     )(
-        core, adapter_down, adapter_up.T, rank_signs_down.T, rank_signs_up.T,
-        width_signs_up.T, width_signs_down.T,
+        *map(pin, (
+            adapter_down, adapter_up.T, rank_signs_down.T, rank_signs_up.T,
+            width_signs_up.T, width_signs_down.T,
+        ))
     )
     blocks = jnp.broadcast_to(block.astype(jnp.float16), (ny * nx, tall, both))
     gathered = lax.all_to_all(blocks, ("y", "x"), 0, 0)
@@ -278,7 +285,7 @@
         scratch_shapes=[pltpu.SemaphoreType.DMA((4,))],
         compiler_params=params(60),
         name="pick",
-    )(core, *sequences)
+    )(core, *map(pin, sequences))
     swap = [(0, 1), (1, 0)]
     recv = lax.ppermute(send, "c", swap)
 
@@ -336,13 +343,13 @@
 
     partial = pl.pallas_call(
         functools.partial(influence_kernel, share=share, slots=nc * ny),
-        out_shape=shape((mates * 8, nz * nc * ny)),
+        out_shape=shape((mates, 1, nz * nc * ny)),
         in_specs=[SMEM, VMEM, VMEM],
         out_specs=VMEM,
         compiler_params=params(16),
         name="partial_influence",
     )(slot, in_plane, held_every.reshape(nz * rows, both))
-    back = lax.all_to_all(partial.reshape(mates, 8, nz * nc * ny), PLANE, 0, 0)
+    back = lax.all_to_all(partial, PLANE, 0, 0)
     influence = jnp.sum(back, axis=(0, 1)).reshape(1, -1) * (1.0 / math.sqrt(half * both))
     return features.reshape(1, half * both), influence
 

time: 95 us -> 92.7 us (0.976)
  no operation moved by 1% of the time
where the time goes in v3:
time: 92.7 us; the launch traced here: 92.2 us
  starting transfers between devices  37 us (40%)
  waiting for transfers between devices  35.6 us (38%)
  Pallas kernels  10.1 us (11%)
  blocking collectives  6.03 us (7%)
  local copies, waits for them, and re-layouts  1.98 us (2%)
    all_to_all x1, starting transfers between devices, shards(): held_every = lax.all_to_all(to_z, 'z', 0, 0)  15.1 us
    all_to_all x1, waiting for transfers between devices, shards(): held_every = lax.all_to_all(to_z, 'z', 0, 0)  11.6 us
    all_to_all x1, waiting for transfers between devices, shards(): gathered = lax.all_to_all(blocks, ('y', 'x'), 0, 0)  9.07 us
    all_to_all x1, waiting for transfers between devices, shards(): in_plane = lax.all_to_all(to_plane, PLANE, 0, 0)  9.01 us
    all_to_all x1, starting transfers between devices, shards(): gathered = lax.all_to_all(blocks, ('y', 'x'), 0, 0)  7.58 us
    all_gather x1, blocking collectives, shards(): pair = lax.all_gather(other, 'c')  6.03 us
    all_to_all x1, waiting for transfers between devices, shards(): back = lax.all_to_all(partial, PLANE, 0, 0)  5.95 us
    all_to_all x1, starting transfers between devices, shards(): back = lax.all_to_all(partial, PLANE, 0, 0)  5.52 us
  transfers between devices with their start and end apart: 5, of which 4 were waited for; matrix products, arithmetic and copies ran while one was open for 1% of the time, Pallas kernels for 5%

profile of v3, /device:TPU:1, one launch (start us, length us, event | category | flops | bytes accessed | tf_op | source)
XLA Modules:
  0.0 92.2 jit_solution(5214613512295563294)
XLA Ops:
  0.6 1.2 %prepare.1 = f32[328,128]{1,0:T(8,128)S(1)} custom-call(bf16[320,128]{1,0:T(8,128)(2,1)} %down_ref.1, bf16[320,128]{1,0:T(8,128)(2,1)} %bitcast.23, bf16[64,128]{1,0:T(8,128)(2,1)} %bitcast.26, bf16[64,128]{1,0:T(8,128)(2,1)} %bitcast.27, bf16[64,320]{1,0:T(8,128)(2,1)} %bitcast.24, bf16[64,320]{1,0:T(8,128)(2,1)} %bitcast.25), custom_call_target="tpu_custom_call" | custom-call | tf_op jit(solution)/shard_map/prepare/pallas_call | solution.py:259
  1.8 1.3 %broadcast_in_dim.3 = f16[16,328,128]{2,1,0:T(8,128)(2,1)} broadcast(f16[328,128]{1,0:T(8,128)(2,1)S(1)} %convert_element_type.6), dimensions={1,2} | broadcast | bytes 1427456 | tf_op jit(solution)/shard_map/broadcast_in_dim | solution.py:278
  3.1 7.6 %all-to-all-start = ((f16[16,328,128]{2,1,0:T(8,128)(2,1)}), f16[16,328,128]{2,1,0:T(8,128)(2,1)S(1)}, u32[]{:S(2)}, u32[]{:S(2)}) async-start(f16[16,328,128]{2,1,0:T(8,128)(2,1)} %broadcast_in_dim.3), calls=%async_computation | async-start | bytes 2686976 | tf_op jit(solution)/shard_map/all_to_all | solution.py:279
  10.7 3.6 %pick.1 = (bf16[160,5120]{1,0:T(8,128)(2,1)}, bf16[160,5120]{1,0:T(8,128)(2,1)}) custom-call(s32[1]{0:T(128)} %bitcast.core_ref, bf16[128,5120]{1,0:T(8,128)(2,1)} %bitcast.19, bf16[128,5120]{1,0:T(8,128)(2,1)} %bitcast.20, bf16[32,5120]{1,0:T(8,128)(2,1)} %bitcast.21, bf16[32,5120]{1,0:T(8,128)(2,1)} %bitcast.22), custom_call_target="tpu_custom_call" | custom-call | tf_op jit(solution)/shard_map/pick/pallas_call | solution.py:280
  14.3 4.9 %collective-permute-start = (bf16[160,5120]{1,0:T(8,128)(2,1)}, bf16[160,5120]{1,0:T(8,128)(2,1)S(1)}, u32[]{:S(2)}, u32[]{:S(2)}) collective-permute-start(bf16[160,5120]{1,0:T(8,128)(2,1)} %get-tuple-element.11), channel_id=1, source_target_pairs={{0,16},{16,0},{1,17},{17,1},{2,18},{18,2},{3,19},{19,3},{4,20},{20... | collective-permute-start | bytes 4915208 | tf_op jit(solution)/shard_map/ppermute | solution.py:290
  19.2 9.1 %all-to-all-done = f16[16,328,128]{2,1,0:T(8,128)(2,1)S(1)} async-done(((f16[16,328,128]{2,1,0:T(8,128)(2,1)}), f16[16,328,128]{2,1,0:T(8,128)(2,1)S(1)}, u32[]{:S(2)}, u32[]{:S(2)}) %all-to-all-start) | async-done | bytes 1343520 | tf_op jit(solution)/shard_map/all_to_all | solution.py:279
  28.2 0.2 convert_element_type.7.values_ref
  28.4 0.6 decode.1.factor_ref
  29.0 0.0 copy-start
  29.0 0.0 collective-permute-done.rows_ref
  29.0 0.6 products.2
  29.6 6.0 %all-gather = f32[256,128]{1,0:T(8,128)S(1)} all-gather(f32[128,128]{1,0:T(8,128)S(1)} %get-tuple-element.14), channel_id=2, replica_groups=mesh['z'=16,'c'=2,'y'=4,'x'=4] {'c'}, dimensions={0}, use_global_device_ids=true | all-gather | bytes 196608 | tf_op jit(solution)/shard_map/all_gather | solution.py:313
  35.6 0.0 copy-done
  35.6 0.6 products.3
  36.2 1.1 %spread.1 = (bf16[32,32,128]{2,1,0:T(8,128)(2,1)}, f32[8,128]{1,0:T(8,128)S(1)}) custom-call(s32[1]{0:T(128)} %bitcast.core_ref, f32[128,128]{1,0:T(8,128)S(1)} %get-tuple-element.13.own_ref, f32[2,128,128]{2,1,0:T(8,128)S(1)} %bitcast.16, f32[32,128]{1,0:T(8,128)S(1)} %get-tuple-element.15.held_own_ref, f32[32,128]{1,0:T(8,128)S(1)} %get-tuple-element.12.refs_0_.held_other_ref), custom_call_target="tpu_custom_call" | custom-call | tf_op jit(solution)/shard_map/spread/pallas_call | solution.py:315
  37.4 3.9 %all-to-all-start.1 = ((bf16[32,32,128]{2,1,0:T(8,128)(2,1)}), bf16[32,32,128]{2,1,0:T(8,128)(2,1)S(1)}, u32[]{:S(2)}, u32[]{:S(2)}) async-start(bf16[32,32,128]{2,1,0:T(8,128)(2,1)} %get-tuple-element.17), calls=%async_computation.1 | async-start | bytes 524288 | tf_op jit(solution)/shard_map/all_to_all | solution.py:331
  41.2 9.0 %all-to-all-done.1.tokens_ref = bf16[32,32,128]{2,1,0:T(8,128)(2,1)S(1)} async-done(((bf16[32,32,128]{2,1,0:T(8,128)(2,1)}), bf16[32,32,128]{2,1,0:T(8,128)(2,1)S(1)}, u32[]{:S(2)}, u32[]{:S(2)}) %all-to-all-start.1) | async-done | bytes 262176 | tf_op jit(solution)/shard_map/all_to_all | solution.py:331
  50.2 1.0 %held_features.1 = bf16[16,16,128]{2,1,0:T(8,128)(2,1)} custom-call(s32[1]{0:T(128)} %bitcast.12.part_ref, bf16[32,32,128]{2,1,0:T(8,128)(2,1)S(1)} %all-to-all-done.1.tokens_ref), custom_call_target="tpu_custom_call" | custom-call | tf_op jit(solution)/shard_map/held_features/pallas_call | solution.py:333
  51.3 15.1 %all-to-all-start.2 = ((bf16[16,16,128]{2,1,0:T(8,128)(2,1)}), bf16[16,16,128]{2,1,0:T(8,128)(2,1)S(1)}, u32[]{:S(2)}, u32[]{:S(2)}) async-start(bf16[16,16,128]{2,1,0:T(8,128)(2,1)} %held_features.1), calls=%async_computation.2 | async-start | bytes 131072 | tf_op jit(solution)/shard_map/all_to_all | solution.py:342
  66.4 11.6 %all-to-all-done.2 = bf16[16,16,128]{2,1,0:T(8,128)(2,1)S(1)} async-done(((bf16[16,16,128]{2,1,0:T(8,128)(2,1)}), bf16[16,16,128]{2,1,0:T(8,128)(2,1)S(1)}, u32[]{:S(2)}, u32[]{:S(2)}) %all-to-all-start.2) | async-done | bytes 65568 | tf_op jit(solution)/shard_map/all_to_all | solution.py:342
  78.0 1.1 %partial_influence.1 = f32[32,1,128]{2,1,0:T(1,128)} custom-call(s32[1]{0:T(128)} %bitcast.11.slot_ref, bf16[32,32,128]{2,1,0:T(8,128)(2,1)S(1)} %all-to-all-done.1.tokens_ref, bf16[256,128]{1,0:T(8,128)(2,1)S(1)} %bitcast.18), custom_call_target="tpu_custom_call" | custom-call | tf_op jit(solution)/shard_map/partial_influence/pallas_call | solution.py:344
  79.1 5.5 %all-to-all-start.3 = ((f32[32,1,128]{2,1,0:T(1,128)}), f32[32,1,128]{2,1,0:T(1,128)S(1)}, u32[]{:S(2)}, u32[]{:S(2)}) async-start(f32[32,1,128]{2,1,0:T(1,128)} %partial_influence.1), calls=%async_computation.3 | async-start | bytes 32768 | tf_op jit(solution)/shard_map/all_to_all | solution.py:352
  84.6 0.4 train_features.1
  85.0 0.7 reshape.47
  85.7 5.9 %all-to-all-done.3 = f32[32,1,128]{2,1,0:T(1,128)S(1)} async-done(((f32[32,1,128]{2,1,0:T(1,128)}), f32[32,1,128]{2,1,0:T(1,128)S(1)}, u32[]{:S(2)}, u32[]{:S(2)}) %all-to-all-start.3) | async-done | bytes 16416 | tf_op jit(solution)/shard_map/all_to_all | solution.py:352
  91.6 0.1 reduce_sum.9
  91.7 0.5 multiply_bitcast_fusion
  (1 shorter events, 0.0 us)
Async XLA Ops:
  3.1 25.2 %all-to-all-start = ((f16[16,328,128]{2,1,0:T(8,128)(2,1)}), f16[16,328,128]{2,1,0:T(8,128)(2,1)S(1)}, u32[]{:S(2)}, u32[]{:S(2)}) async-start(f16[16,328,128]{2,1,0:T(8,128)(2,1)} %broadcast_in_dim.3), calls=%async_computation | async-start | bytes 2686976 | tf_op jit(solution)/shard_map/all_to_all | solution.py:279
  14.3 14.7 %collective-permute-start = (bf16[160,5120]{1,0:T(8,128)(2,1)}, bf16[160,5120]{1,0:T(8,128)(2,1)S(1)}, u32[]{:S(2)}, u32[]{:S(2)}) collective-permute-start(bf16[160,5120]{1,0:T(8,128)(2,1)} %get-tuple-element.11), channel_id=1, source_target_pairs={{0,16},{16,0},{1,17},{17,1},{2,18},{18,2},{3,19},{19,3},{4,20},{20... | collective-permute-start | bytes 4915208 | tf_op jit(solution)/shard_map/ppermute | solution.py:290
  29.0 6.7 %copy-start = (bf16[160,5120]{1,0:T(8,128)(2,1)S(1)}, bf16[160,5120]{1,0:T(8,128)(2,1)}, u32[]{:S(2)}) copy-start(bf16[160,5120]{1,0:T(8,128)(2,1)} %get-tuple-element.10.rows_ref) | copy-start | bytes 4915204
  37.4 12.9 %all-to-all-start.1 = ((bf16[32,32,128]{2,1,0:T(8,128)(2,1)}), bf16[32,32,128]{2,1,0:T(8,128)(2,1)S(1)}, u32[]{:S(2)}, u32[]{:S(2)}) async-start(bf16[32,32,128]{2,1,0:T(8,128)(2,1)} %get-tuple-element.17), calls=%async_computation.1 | async-start | bytes 524288 | tf_op jit(solution)/shard_map/all_to_all | solution.py:331
  51.3 26.7 %all-to-all-start.2 = ((bf16[16,16,128]{2,1,0:T(8,128)(2,1)}), bf16[16,16,128]{2,1,0:T(8,128)(2,1)S(1)}, u32[]{:S(2)}, u32[]{:S(2)}) async-start(bf16[16,16,128]{2,1,0:T(8,128)(2,1)} %held_features.1), calls=%async_computation.2 | async-start | bytes 131072 | tf_op jit(solution)/shard_map/all_to_all | solution.py:342
  79.1 12.6 %all-to-all-start.3 = ((f32[32,1,128]{2,1,0:T(1,128)}), f32[32,1,128]{2,1,0:T(1,128)S(1)}, u32[]{:S(2)}, u32[]{:S(2)}) async-start(f32[32,1,128]{2,1,0:T(1,128)} %partial_influence.1), calls=%async_computation.3 | async-start | bytes 32768 | tf_op jit(solution)/shard_map/all_to_all | solution.py:352

commit v4 on v3

--- a/solution.py
+++ b/solution.py
@@ -82,8 +82,8 @@
     block_ref[pl.ds(rows, EXTRA), :] = jnp.broadcast_to(exponent, (EXTRA, 2 * half))
 
 
-def pick_kernel(core_ref, xt_ref, gt_ref, xh_ref, gh_ref, keep_ref, send_ref, sems):
-    first = core_ref[0] == 0
+def pick_kernel(xt_ref, gt_ref, xh_ref, gh_ref, keep_ref, send_ref, sems):
+    first = lax.axis_index("c") == 0
     tokens = xt_ref.shape[0]
     held = xh_ref.shape[0]
 
@@ -133,6 +133,20 @@
     held_ref[...] = value[tokens:]
 
 
+def halves(value):
+    high = value.astype(jnp.bfloat16)
+    return high, (value - high.astype(jnp.float32)).astype(jnp.bfloat16)
+
+
+def stacked(a, b):
+    a_high, a_low = halves(a)
+    b_high, b_low = halves(b)
+    return tn(
+        jnp.concatenate([a_high, a_high, a_low], axis=0),
+        jnp.concatenate([b_high, b_low, b_high], axis=0),
+    )
+
+
 def joined(product, half):
     lane = lax.broadcasted_iota(jnp.int32, (half, 2 * half), 1)
     return jnp.where(lane < half, product[:half], product[half:])
@@ -142,17 +156,17 @@
     return lax.rsqrt(jnp.sum(values * values, keepdims=True) * (1.0 / values.size) + EPSILON)
 
 
-def kinds(core_ref, own_ref, pair_ref):
-    first = core_ref[0] == 0
+def kinds(own_ref, pair_ref):
+    first = lax.axis_index("c") == 0
     own = own_ref[...]
     return jnp.where(first, own, pair_ref[0]), jnp.where(first, pair_ref[1], own)
 
 
 def spread_kernel(
-    core_ref, own_ref, pair_ref, held_own_ref, held_other_ref, out_ref, scale_ref, *, share, copies
+    own_ref, pair_ref, held_own_ref, held_other_ref, out_ref, scale_ref, *, share, copies
 ):
-    of_g, of_x = kinds(core_ref, own_ref, pair_ref)
-    product = tn(of_x, of_g, HIGH)
+    of_g, of_x = kinds(own_ref, pair_ref)
+    product = stacked(of_x, of_g)
     half = product.shape[0] // 2
     values = joined(product, half)
     scale = scale_of(values)
@@ -160,7 +174,7 @@
     rounded = (values * scale).astype(jnp.bfloat16)
     rows = half // copies
     groups = out_ref.shape[0] // (2 * copies)
-    first = core_ref[0] == 0
+    first = lax.axis_index("c") == 0
     own, other = held_own_ref[...], held_other_ref[...]
     for c, held in enumerate((jnp.where(first, own, other), jnp.where(first, other, own))):
         high = held.astype(jnp.bfloat16).astype(jnp.float32)
@@ -174,33 +188,35 @@
                 out_ref[i, pl.ds(2 * share, rows), :] = rounded[j * rows : (j + 1) * rows]
 
 
-def feature_kernel(core_ref, own_ref, pair_ref, scale_ref, features_ref):
-    of_g, of_x = kinds(core_ref, own_ref, pair_ref)
+def feature_kernel(own_ref, pair_ref, scale_ref, features_ref):
+    of_g, of_x = kinds(own_ref, pair_ref)
     half = features_ref.shape[1]
     scale = scale_ref[pl.ds(0, 1), :]
     features_ref[0] = (tn(of_x, of_g, HIGH) * scale)[:half, :half].astype(jnp.bfloat16)
     features_ref[1] = (tn(of_g, of_x, HIGH) * scale)[half:, half:].astype(jnp.bfloat16)
 
 
-def normal_kernel(part_ref, tokens_ref, out_ref, held_ref, *, share):
+def normal_kernel(tokens_ref, out_ref, held_ref, *, share):
     count = tokens_ref.shape[0] // 2
     both = tokens_ref.shape[2]
     pairs = tokens_ref[:, pl.ds(0, 2 * share), :].astype(jnp.float32)
     tokens = (pairs[:, :share] + pairs[:, share:]).reshape(count, 2, share, both)
     of_g = tokens[:, 0].reshape(count * share, both)
     of_x = tokens[:, 1].reshape(count * share, both)
-    product = tn(of_x, of_g, HIGH)
+    product = stacked(of_x, of_g)
     half = both // 2
     values = joined(product, half)
     held_ref[...] = values * scale_of(values)
     rows = out_ref.shape[1]
-    start = pl.multiple_of(part_ref[0] * rows, rows)
+    start = pl.multiple_of(lax.axis_index("x") * rows, rows)
     own = held_ref[pl.ds(start, rows), :].astype(jnp.bfloat16)
     for i in range(out_ref.shape[0]):
         out_ref[i] = own
 
 
-def influence_kernel(slot_ref, tokens_ref, held_ref, out_ref, *, share, slots):
+def influence_kernel(tokens_ref, held_ref, out_ref, *, share, groups):
+    slots = 2 * groups
+    slot = lax.axis_index("c") * groups + lax.axis_index("y")
     mates, _, both = tokens_ref.shape
     rows = tokens_ref.shape[1] - 2 * share
     train = tokens_ref[:, pl.ds(2 * share, rows), :].reshape(mates * rows, both)
@@ -213,13 +229,16 @@
     summed = jnp.sum(every.reshape(trains, rows, m), axis=1)
     row = lax.broadcasted_iota(jnp.int32, (m, out_ref.shape[2]), 0)
     col = lax.broadcasted_iota(jnp.int32, (m, out_ref.shape[2]), 1)
-    place = jnp.where(col == lax.div(row, rows) * slots + slot_ref[0], 1.0, 0.0)
-    placed = nn(summed, place, HIGH)
+    place = jnp.where(col == lax.div(row, rows) * slots + slot, 1.0, 0.0)
+    high = summed.astype(jnp.bfloat16).astype(jnp.float32)
+    middle = (summed - high).astype(jnp.bfloat16).astype(jnp.float32)
+    terms = jnp.concatenate([high, middle, summed - high - middle], axis=0)
+    terms = nn(terms.astype(jnp.bfloat16), place.astype(jnp.bfloat16))
+    placed = terms[:trains] + terms[trains : 2 * trains] + terms[2 * trains :]
     for i in range(trains):
         out_ref[i] = placed[i : i + 1]
 
 
-SMEM = pl.BlockSpec(memory_space=pltpu.SMEM)
 VMEM = pl.BlockSpec(memory_space=pltpu.VMEM)
 HBM = pl.BlockSpec(memory_space=pl.ANY)
 
@@ -238,9 +257,6 @@
 ):
     nz, nc, ny, nx = sizes
     mates = nc * ny * nx
-    core = lax.axis_index("c").astype(jnp.int32).reshape(1)
-    part = lax.axis_index("x").astype(jnp.int32).reshape(1)
-    slot = (lax.axis_index("c") * ny + lax.axis_index("y")).astype(jnp.int32).reshape(1)
     tokens, width = train_inputs.shape[1:]
     groups, share = held_inputs.shape[:2]
     held_rows = groups * share
@@ -280,12 +296,12 @@
     keep, send = pl.pallas_call(
         pick_kernel,
         out_shape=(shape((tokens + held_rows, width), bf16),) * 2,
-        in_specs=[SMEM] + [HBM] * 4,
+        in_specs=[HBM] * 4,
         out_specs=(VMEM, VMEM),
         scratch_shapes=[pltpu.SemaphoreType.DMA((4,))],
         compiler_params=params(60),
         name="pick",
-    )(core, *map(pin, sequences))
+    )(*map(pin, sequences))
     swap = [(0, 1), (1, 0)]
     recv = lax.ppermute(send, "c", swap)
 
@@ -315,40 +331,40 @@
     to_plane, scale = pl.pallas_call(
         functools.partial(spread_kernel, share=share, copies=nx),
         out_shape=(shape((mates, 2 * share + rows, both), bf16), shape((8, both))),
-        in_specs=[SMEM] + [VMEM] * 4,
+        in_specs=[VMEM] * 4,
         out_specs=(VMEM, VMEM),
         compiler_params=params(40),
         name="spread",
-    )(core, own, pair, held_own, held_other)
+    )(own, pair, held_own, held_other)
     features = pl.pallas_call(
         feature_kernel,
         out_shape=shape((2, half, half), bf16),
-        in_specs=[SMEM] + [VMEM] * 3,
+        in_specs=[VMEM] * 3,
         out_specs=VMEM,
         compiler_params=params(16),
         name="train_features",
-    )(core, own, pair, scale)
+    )(own, pair, scale)
     in_plane = lax.all_to_all(to_plane, PLANE, 0, 0)
 
     to_z = pl.pallas_call(
         functools.partial(normal_kernel, share=share),
         out_shape=shape((nz, rows, both), bf16),
-        in_specs=[SMEM, VMEM],
+        in_specs=[VMEM],
         out_specs=VMEM,
         scratch_shapes=[pltpu.VMEM((half, both), jnp.float32)],
         compiler_params=params(16),
         name="held_features",
-    )(part, in_plane)
+    )(in_plane)
     held_every = lax.all_to_all(to_z, "z", 0, 0)
 
     partial = pl.pallas_call(
-        functools.partial(influence_kernel, share=share, slots=nc * ny),
+        functools.partial(influence_kernel, share=share, groups=ny),
         out_shape=shape((mates, 1, nz * nc * ny)),
-        in_specs=[SMEM, VMEM, VMEM],
+        in_specs=[VMEM, VMEM],
         out_specs=VMEM,
         compiler_params=params(16),
         name="partial_influence",
-    )(slot, in_plane, held_every.reshape(nz * rows, both))
+    )(in_plane, held_every.reshape(nz * rows, both))
     back = lax.all_to_all(partial, PLANE, 0, 0)
     influence = jnp.sum(back, axis=(0, 1)).reshape(1, -1) * (1.0 / math.sqrt(half * both))
     return features.reshape(1, half * both), influence

time: 92.7 us -> 90.3 us (0.974)
  blocking collectives: 6.03 us -> 44.8 us
  waiting for transfers between devices: 35.6 us -> 14.9 us
  starting transfers between devices: 37 us -> 18.1 us
  Pallas kernels: 10.1 us -> 8.66 us
    all_to_all x0 -> x2, blocking collectives: none -> 38.8 us  [the longest x1 26.8 us: shards(): held_every = lax.all_to_all(to_z, 'z', 0, 0)]
    all_to_all x2 -> x0, waiting for transfers between devices: 20.6 us -> none  [the longest x1 11.6 us: shards(): held_every = lax.all_to_all(to_z, 'z', 0, 0)]
    all_to_all x2 -> x0, starting transfers between devices: 19 us -> none  [the longest x1 15.1 us: shards(): held_every = lax.all_to_all(to_z, 'z', 0, 0)]
  transfers between devices with their start and end apart: 5 -> 3, of which waited for: 4 -> 2; matrix products, arithmetic and copies ran while one was open for 1% -> 1% of each run, Pallas kernels for 5% -> 5%
where the time goes in v4:
time: 90.3 us; the launch traced here: 89.9 us
  blocking collectives  44.8 us (50%)
  starting transfers between devices  18.1 us (20%)
  waiting for transfers between devices  14.9 us (17%)
  Pallas kernels  8.66 us (10%)
  local copies, waits for them, and re-layouts  1.97 us (2%)
    all_to_all x1, blocking collectives, shards(): held_every = lax.all_to_all(to_z, 'z', 0, 0)  26.8 us
    all_to_all x1, blocking collectives, shards(): in_plane = lax.all_to_all(to_plane, PLANE, 0, 0)  12 us
    all_to_all x1, waiting for transfers between devices, shards(): gathered = lax.all_to_all(blocks, ('y', 'x'), 0, 0)  9.07 us
    all_to_all x1, starting transfers between devices, shards(): gathered = lax.all_to_all(blocks, ('y', 'x'), 0, 0)  7.58 us
    all_gather x1, blocking collectives, shards(): pair = lax.all_gather(other, 'c')  6.03 us
    all_to_all x1, waiting for transfers between devices, shards(): back = lax.all_to_all(partial, PLANE, 0, 0)  5.83 us
    all_to_all x1, starting transfers between devices, shards(): back = lax.all_to_all(partial, PLANE, 0, 0)  5.57 us
    ppermute x1, starting transfers between devices, shards(): recv = lax.ppermute(send, 'c', swap)  4.9 us
  transfers between devices with their start and end apart: 3, of which 2 were waited for; matrix products, arithmetic and copies ran while one was open for 1% of the time, Pallas kernels for 5%

profile of v4, /device:TPU:1, one launch (start us, length us, event | category | flops | bytes accessed | tf_op | source)
XLA Modules:
  0.0 89.9 jit_solution(11599820380355554183)
XLA Ops:
  0.6 1.2 %prepare.1 = f32[328,128]{1,0:T(8,128)S(1)} custom-call(bf16[320,128]{1,0:T(8,128)(2,1)} %down_ref.1, bf16[320,128]{1,0:T(8,128)(2,1)} %bitcast.20, bf16[64,128]{1,0:T(8,128)(2,1)} %bitcast.23, bf16[64,128]{1,0:T(8,128)(2,1)} %bitcast.24, bf16[64,320]{1,0:T(8,128)(2,1)} %bitcast.21, bf16[64,320]{1,0:T(8,128)(2,1)} %bitcast.22), custom_call_target="tpu_custom_call" | custom-call | tf_op jit(solution)/shard_map/prepare/pallas_call | solution.py:275
  1.8 1.2 %broadcast_in_dim.3 = f16[16,328,128]{2,1,0:T(8,128)(2,1)} broadcast(f16[328,128]{1,0:T(8,128)(2,1)S(1)} %convert_element_type.6), dimensions={1,2} | broadcast | bytes 1427456 | tf_op jit(solution)/shard_map/broadcast_in_dim | solution.py:294
  3.1 7.6 %all-to-all-start = ((f16[16,328,128]{2,1,0:T(8,128)(2,1)}), f16[16,328,128]{2,1,0:T(8,128)(2,1)S(1)}, u32[]{:S(2)}, u32[]{:S(2)}) async-start(f16[16,328,128]{2,1,0:T(8,128)(2,1)} %broadcast_in_dim.3), calls=%async_computation | async-start | bytes 2686976 | tf_op jit(solution)/shard_map/all_to_all | solution.py:295
  10.7 3.6 %pick.1 = (bf16[160,5120]{1,0:T(8,128)(2,1)}, bf16[160,5120]{1,0:T(8,128)(2,1)}) custom-call(bf16[128,5120]{1,0:T(8,128)(2,1)} %bitcast.16, bf16[128,5120]{1,0:T(8,128)(2,1)} %bitcast.17, bf16[32,5120]{1,0:T(8,128)(2,1)} %bitcast.18, bf16[32,5120]{1,0:T(8,128)(2,1)} %bitcast.19), custom_call_target="tpu_custom_call" | custom-call | tf_op jit(solution)/shard_map/pick/pallas_call | solution.py:296
  14.3 4.9 %collective-permute-start = (bf16[160,5120]{1,0:T(8,128)(2,1)}, bf16[160,5120]{1,0:T(8,128)(2,1)S(1)}, u32[]{:S(2)}, u32[]{:S(2)}) collective-permute-start(bf16[160,5120]{1,0:T(8,128)(2,1)} %get-tuple-element.11), channel_id=1, source_target_pairs={{0,16},{16,0},{1,17},{17,1},{2,18},{18,2},{3,19},{19,3},{4,20},{20... | collective-permute-start | bytes 4915208 | tf_op jit(solution)/shard_map/ppermute | solution.py:306
  19.2 9.1 %all-to-all-done = f16[16,328,128]{2,1,0:T(8,128)(2,1)S(1)} async-done(((f16[16,328,128]{2,1,0:T(8,128)(2,1)}), f16[16,328,128]{2,1,0:T(8,128)(2,1)S(1)}, u32[]{:S(2)}, u32[]{:S(2)}) %all-to-all-start) | async-done | bytes 1343520 | tf_op jit(solution)/shard_map/all_to_all | solution.py:295
  28.2 0.2 convert_element_type.7.values_ref
  28.4 0.6 decode.1.factor_ref
  29.0 0.0 copy-start
  29.0 0.0 collective-permute-done.rows_ref
  29.0 0.6 products.2
  29.6 6.0 %all-gather = f32[256,128]{1,0:T(8,128)S(1)} all-gather(f32[128,128]{1,0:T(8,128)S(1)} %get-tuple-element.14), channel_id=2, replica_groups=mesh['z'=16,'c'=2,'y'=4,'x'=4] {'c'}, dimensions={0}, use_global_device_ids=true | all-gather | bytes 196608 | tf_op jit(solution)/shard_map/all_gather | solution.py:329
  35.6 0.0 copy-done
  35.6 0.6 products.3
  36.2 0.4 spread.1
  36.6 12.0 %all_to_all.20.tokens_ref = bf16[32,32,128]{2,1,0:T(8,128)(2,1)S(1)} all-to-all(bf16[32,32,128]{2,1,0:T(8,128)(2,1)S(1)} %get-tuple-element.17), channel_id=1, replica_groups=mesh['z'=16,'c'=2,'y'=4,'x'=4] {'y','x','c'}, dimensions={0} | all-to-all | bytes 524288 | tf_op jit(solution)/shard_map/all_to_all | solution.py:347
  48.6 0.3 held_features.1
  49.0 26.8 %all_to_all.21 = bf16[16,16,128]{2,1,0:T(8,128)(2,1)S(1)} all-to-all(bf16[16,16,128]{2,1,0:T(8,128)(2,1)S(1)} %held_features.1), channel_id=1, replica_groups=mesh['z'=16,'c'=2,'y'=4,'x'=4] {'z'}, dimensions={0} | all-to-all | bytes 131072 | tf_op jit(solution)/shard_map/all_to_all | solution.py:358
  75.8 1.1 %partial_influence.1 = f32[32,1,128]{2,1,0:T(1,128)} custom-call(bf16[32,32,128]{2,1,0:T(8,128)(2,1)S(1)} %all_to_all.20.tokens_ref, bf16[256,128]{1,0:T(8,128)(2,1)S(1)} %bitcast.15), custom_call_target="tpu_custom_call" | custom-call | tf_op jit(solution)/shard_map/partial_influence/pallas_call | solution.py:360
  76.8 5.6 %all-to-all-start.3 = ((f32[32,1,128]{2,1,0:T(1,128)}), f32[32,1,128]{2,1,0:T(1,128)S(1)}, u32[]{:S(2)}, u32[]{:S(2)}) async-start(f32[32,1,128]{2,1,0:T(1,128)} %partial_influence.1), calls=%async_computation.3 | async-start | bytes 32768 | tf_op jit(solution)/shard_map/all_to_all | solution.py:368
  82.4 0.4 train_features.1
  82.8 0.7 reshape.37
  83.5 5.8 %all-to-all-done.3 = f32[32,1,128]{2,1,0:T(1,128)S(1)} async-done(((f32[32,1,128]{2,1,0:T(1,128)}), f32[32,1,128]{2,1,0:T(1,128)S(1)}, u32[]{:S(2)}, u32[]{:S(2)}) %all-to-all-start.3) | async-done | bytes 16416 | tf_op jit(solution)/shard_map/all_to_all | solution.py:368
  89.4 0.1 reduce_sum.9
  89.4 0.5 multiply_bitcast_fusion
  (1 shorter events, 0.0 us)
Async XLA Ops:
  3.1 25.2 %all-to-all-start = ((f16[16,328,128]{2,1,0:T(8,128)(2,1)}), f16[16,328,128]{2,1,0:T(8,128)(2,1)S(1)}, u32[]{:S(2)}, u32[]{:S(2)}) async-start(f16[16,328,128]{2,1,0:T(8,128)(2,1)} %broadcast_in_dim.3), calls=%async_computation | async-start | bytes 2686976 | tf_op jit(solution)/shard_map/all_to_all | solution.py:295
  14.3 14.7 %collective-permute-start = (bf16[160,5120]{1,0:T(8,128)(2,1)}, bf16[160,5120]{1,0:T(8,128)(2,1)S(1)}, u32[]{:S(2)}, u32[]{:S(2)}) collective-permute-start(bf16[160,5120]{1,0:T(8,128)(2,1)} %get-tuple-element.11), channel_id=1, source_target_pairs={{0,16},{16,0},{1,17},{17,1},{2,18},{18,2},{3,19},{19,3},{4,20},{20... | collective-permute-start | bytes 4915208 | tf_op jit(solution)/shard_map/ppermute | solution.py:306
  29.0 6.7 %copy-start = (bf16[160,5120]{1,0:T(8,128)(2,1)S(1)}, bf16[160,5120]{1,0:T(8,128)(2,1)}, u32[]{:S(2)}) copy-start(bf16[160,5120]{1,0:T(8,128)(2,1)} %get-tuple-element.10.rows_ref) | copy-start | bytes 4915204
  76.8 12.5 %all-to-all-start.3 = ((f32[32,1,128]{2,1,0:T(1,128)}), f32[32,1,128]{2,1,0:T(1,128)S(1)}, u32[]{:S(2)}, u32[]{:S(2)}) async-start(f32[32,1,128]{2,1,0:T(1,128)} %partial_influence.1), calls=%async_computation.3 | async-start | bytes 32768 | tf_op jit(solution)/shard_map/all_to_all | solution.py:368

commit v5 on v4

--- a/solution.py
+++ b/solution.py
@@ -163,14 +163,18 @@
 
 
 def spread_kernel(
-    own_ref, pair_ref, held_own_ref, held_other_ref, out_ref, scale_ref, *, share, copies
+    own_ref, pair_ref, held_own_ref, held_other_ref, out_ref, features_ref, *, share, copies
 ):
     of_g, of_x = kinds(own_ref, pair_ref)
     product = stacked(of_x, of_g)
     half = product.shape[0] // 2
     values = joined(product, half)
     scale = scale_of(values)
-    scale_ref[...] = jnp.broadcast_to(scale, scale_ref.shape)
+    lane = lax.broadcasted_iota(jnp.int32, (half, 2 * half), 1)
+    up = jnp.where(lane < half, product[:half] * scale, 0.0).astype(jnp.bfloat16)
+    turned = stacked(of_g, of_x)
+    down = jnp.where(lane < half, 0.0, turned[half:] * scale).astype(jnp.bfloat16)
+    features_ref[...] = jnp.concatenate([paired(up, False), paired(down, True)], axis=0)
     rounded = (values * scale).astype(jnp.bfloat16)
     rows = half // copies
     groups = out_ref.shape[0] // (2 * copies)
@@ -188,12 +192,15 @@
                 out_ref[i, pl.ds(2 * share, rows), :] = rounded[j * rows : (j + 1) * rows]
 
 
-def feature_kernel(own_ref, pair_ref, scale_ref, features_ref):
-    of_g, of_x = kinds(own_ref, pair_ref)
-    half = features_ref.shape[1]
-    scale = scale_ref[pl.ds(0, 1), :]
-    features_ref[0] = (tn(of_x, of_g, HIGH) * scale)[:half, :half].astype(jnp.bfloat16)
-    features_ref[1] = (tn(of_g, of_x, HIGH) * scale)[half:, half:].astype(jnp.bfloat16)
+def paired(values, at_right):
+    rows, lanes = values.shape
+    row = lax.broadcasted_iota(jnp.int32, (rows // 2, rows), 0)
+    col = lax.broadcasted_iota(jnp.int32, (rows // 2, rows), 1)
+    even = nn(jnp.where(col == 2 * row, 1.0, 0.0).astype(jnp.bfloat16), values)
+    odd = nn(jnp.where(col == 2 * row + 1, 1.0, 0.0).astype(jnp.bfloat16), values)
+    if at_right:
+        return pltpu.roll(even, lanes // 2, 1) + odd
+    return even + pltpu.roll(odd, lanes // 2, 1)
 
 
 def normal_kernel(tokens_ref, out_ref, held_ref, *, share):
@@ -239,6 +246,17 @@
         out_ref[i] = placed[i : i + 1]
 
 
+def final_kernel(back_ref, flat_ref, features_ref, influence_ref, *, factor):
+    total = back_ref[0]
+    for i in range(1, back_ref.shape[0]):
+        total += back_ref[i]
+    influence_ref[...] = total * factor
+    rows, lanes = flat_ref.shape
+    flat = flat_ref[...].astype(jnp.bfloat16)
+    for i in range(rows):
+        features_ref[:, pl.ds(i * lanes, lanes)] = flat[i : i + 1]
+
+
 VMEM = pl.BlockSpec(memory_space=pltpu.VMEM)
 HBM = pl.BlockSpec(memory_space=pl.ANY)
 
@@ -328,22 +346,14 @@
     own, held_own = products(factor, keep, held_other)
     pair = lax.all_gather(other, "c")
 
-    to_plane, scale = pl.pallas_call(
+    to_plane, features = pl.pallas_call(
         functools.partial(spread_kernel, share=share, copies=nx),
-        out_shape=(shape((mates, 2 * share + rows, both), bf16), shape((8, both))),
+        out_shape=(shape((mates, 2 * share + rows, both), bf16), shape((half, both))),
         in_specs=[VMEM] * 4,
         out_specs=(VMEM, VMEM),
         compiler_params=params(40),
         name="spread",
     )(own, pair, held_own, held_other)
-    features = pl.pallas_call(
-        feature_kernel,
-        out_shape=shape((2, half, half), bf16),
-        in_specs=[VMEM] * 3,
-        out_specs=VMEM,
-        compiler_params=params(16),
-        name="train_features",
-    )(own, pair, scale)
     in_plane = lax.all_to_all(to_plane, PLANE, 0, 0)
 
     to_z = pl.pallas_call(
@@ -366,8 +376,15 @@
         name="partial_influence",
     )(in_plane, held_every.reshape(nz * rows, both))
     back = lax.all_to_all(partial, PLANE, 0, 0)
-    influence = jnp.sum(back, axis=(0, 1)).reshape(1, -1) * (1.0 / math.sqrt(half * both))
-    return features.reshape(1, half * both), influence
+    features, influence = pl.pallas_call(
+        functools.partial(final_kernel, factor=1.0 / math.sqrt(half * both)),
+        out_shape=(shape((1, half * both), bf16), shape((1, nz * nc * ny))),
+        in_specs=[VMEM, VMEM],
+        out_specs=(VMEM, VMEM),
+        compiler_params=params(16),
+        name="final",
+    )(back, features)
+    return features, influence
 
 
 def solution(mesh):

time: 90.3 us -> 89.8 us (level)
  blocking collectives: 44.8 us -> 57.1 us
  waiting for transfers between devices: 14.9 us -> 9.07 us
  starting transfers between devices: 18.1 us -> 12.5 us
    all_to_all x0 -> x1, blocking collectives: none -> 12.3 us  [shards(): back = lax.all_to_all(partial, PLANE, 0, 0)]
    all_to_all x1 -> x0, waiting for transfers between devices: 5.83 us -> none  [shards(): back = lax.all_to_all(partial, PLANE, 0, 0)]
    all_to_all x1 -> x0, starting transfers between devices: 5.57 us -> none  [shards(): back = lax.all_to_all(partial, PLANE, 0, 0)]
  transfers between devices with their start and end apart: 3 -> 2, of which waited for: 2 -> 1; matrix products, arithmetic and copies ran while one was open for 1% -> 0% of each run, Pallas kernels for 5% -> 5%
where the time goes in v5:
time: 89.8 us; the launch traced here: 89.4 us
  blocking collectives  57.1 us (64%)
  starting transfers between devices  12.5 us (14%)
  waiting for transfers between devices  9.07 us (10%)
  Pallas kernels  8.52 us (9%)
  local copies, waits for them, and re-layouts  1.25 us (1%)
    all_to_all x1, blocking collectives, shards(): held_every = lax.all_to_all(to_z, 'z', 0, 0)  26.8 us
    all_to_all x1, blocking collectives, shards(): back = lax.all_to_all(partial, PLANE, 0, 0)  12.3 us
    all_to_all x1, blocking collectives, shards(): in_plane = lax.all_to_all(to_plane, PLANE, 0, 0)  12 us
    all_to_all x1, waiting for transfers between devices, shards(): gathered = lax.all_to_all(blocks, ('y', 'x'), 0, 0)  9.07 us
    all_to_all x1, starting transfers between devices, shards(): gathered = lax.all_to_all(blocks, ('y', 'x'), 0, 0)  7.58 us
    all_gather x1, blocking collectives, shards(): pair = lax.all_gather(other, 'c')  6.03 us
    ppermute x1, starting transfers between devices, shards(): recv = lax.ppermute(send, 'c', swap)  4.9 us
    pallas_call x1, Pallas kernels, shards(): pl.pallas_call(pick_kernel, out_shape=(shape((tokens + held_rows, width),...  3.59 us
  transfers between devices with their start and end apart: 2, of which 1 were waited for; matrix products, arithmetic and copies ran while one was open for 0% of the time, Pallas kernels for 5%

profile of v5, /device:TPU:1, one launch (start us, length us, event | category | flops | bytes accessed | tf_op | source)
XLA Modules:
  0.0 89.4 jit_solution(17344464495669232051)
XLA Ops:
  0.6 1.2 %prepare.1 = f32[328,128]{1,0:T(8,128)S(1)} custom-call(bf16[320,128]{1,0:T(8,128)(2,1)} %down_ref.1, bf16[320,128]{1,0:T(8,128)(2,1)} %bitcast.17, bf16[64,128]{1,0:T(8,128)(2,1)} %bitcast.20, bf16[64,128]{1,0:T(8,128)(2,1)} %bitcast.21, bf16[64,320]{1,0:T(8,128)(2,1)} %bitcast.18, bf16[64,320]{1,0:T(8,128)(2,1)} %bitcast.19), custom_call_target="tpu_custom_call" | custom-call | tf_op jit(solution)/shard_map/prepare/pallas_call | solution.py:293
  1.8 1.2 %broadcast_in_dim.3 = f16[16,328,128]{2,1,0:T(8,128)(2,1)} broadcast(f16[328,128]{1,0:T(8,128)(2,1)S(1)} %convert_element_type.6), dimensions={1,2} | broadcast | bytes 1427456 | tf_op jit(solution)/shard_map/broadcast_in_dim | solution.py:312
  3.1 7.6 %all-to-all-start = ((f16[16,328,128]{2,1,0:T(8,128)(2,1)}), f16[16,328,128]{2,1,0:T(8,128)(2,1)S(1)}, u32[]{:S(2)}, u32[]{:S(2)}) async-start(f16[16,328,128]{2,1,0:T(8,128)(2,1)} %broadcast_in_dim.3), calls=%async_computation | async-start | bytes 2686976 | tf_op jit(solution)/shard_map/all_to_all | solution.py:313
  10.7 3.6 %pick.1 = (bf16[160,5120]{1,0:T(8,128)(2,1)}, bf16[160,5120]{1,0:T(8,128)(2,1)}) custom-call(bf16[128,5120]{1,0:T(8,128)(2,1)} %bitcast.13, bf16[128,5120]{1,0:T(8,128)(2,1)} %bitcast.14, bf16[32,5120]{1,0:T(8,128)(2,1)} %bitcast.15, bf16[32,5120]{1,0:T(8,128)(2,1)} %bitcast.16), custom_call_target="tpu_custom_call" | custom-call | tf_op jit(solution)/shard_map/pick/pallas_call | solution.py:314
  14.3 4.9 %collective-permute-start = (bf16[160,5120]{1,0:T(8,128)(2,1)}, bf16[160,5120]{1,0:T(8,128)(2,1)S(1)}, u32[]{:S(2)}, u32[]{:S(2)}) collective-permute-start(bf16[160,5120]{1,0:T(8,128)(2,1)} %get-tuple-element.11), channel_id=1, source_target_pairs={{0,16},{16,0},{1,17},{17,1},{2,18},{18,2},{3,19},{19,3},{4,20},{20... | collective-permute-start | bytes 4915208 | tf_op jit(solution)/shard_map/ppermute | solution.py:324
  19.2 9.1 %all-to-all-done = f16[16,328,128]{2,1,0:T(8,128)(2,1)S(1)} async-done(((f16[16,328,128]{2,1,0:T(8,128)(2,1)}), f16[16,328,128]{2,1,0:T(8,128)(2,1)S(1)}, u32[]{:S(2)}, u32[]{:S(2)}) %all-to-all-start) | async-done | bytes 1343520 | tf_op jit(solution)/shard_map/all_to_all | solution.py:313
  28.2 0.2 convert_element_type.7.values_ref
  28.4 0.6 decode.1.factor_ref
  29.0 0.0 copy-start
  29.0 0.0 collective-permute-done.rows_ref
  29.0 0.6 products.2
  29.6 6.0 %all-gather = f32[256,128]{1,0:T(8,128)S(1)} all-gather(f32[128,128]{1,0:T(8,128)S(1)} %get-tuple-element.14), channel_id=2, replica_groups=mesh['z'=16,'c'=2,'y'=4,'x'=4] {'c'}, dimensions={0}, use_global_device_ids=true | all-gather | bytes 196608 | tf_op jit(solution)/shard_map/all_gather | solution.py:347
  35.6 0.0 copy-done
  35.6 0.6 products.3
  36.2 0.6 spread.1
  36.8 12.0 %all_to_all.20.tokens_ref = bf16[32,32,128]{2,1,0:T(8,128)(2,1)S(1)} all-to-all(bf16[32,32,128]{2,1,0:T(8,128)(2,1)S(1)} %get-tuple-element.16), channel_id=1, replica_groups=mesh['z'=16,'c'=2,'y'=4,'x'=4] {'y','x','c'}, dimensions={0} | all-to-all | bytes 524288 | tf_op jit(solution)/shard_map/all_to_all | solution.py:357
  48.8 0.3 held_features.1
  49.2 26.8 %all_to_all.21 = bf16[16,16,128]{2,1,0:T(8,128)(2,1)S(1)} all-to-all(bf16[16,16,128]{2,1,0:T(8,128)(2,1)S(1)} %held_features.1), channel_id=1, replica_groups=mesh['z'=16,'c'=2,'y'=4,'x'=4] {'z'}, dimensions={0} | all-to-all | bytes 131072 | tf_op jit(solution)/shard_map/all_to_all | solution.py:368
  76.0 0.5 partial_influence.1
  76.4 12.3 %all_to_all.22.back_ref = f32[32,1,128]{2,1,0:T(1,128)S(1)} all-to-all(f32[32,1,128]{2,1,0:T(1,128)S(1)} %partial_influence.1), channel_id=1, replica_groups=mesh['z'=16,'c'=2,'y'=4,'x'=4] {'y','x','c'}, dimensions={0} | all-to-all | bytes 32768 | tf_op jit(solution)/shard_map/all_to_all | solution.py:378
  88.7 0.7 final.1
  (1 shorter events, 0.0 us)
Async XLA Ops:
  3.1 25.2 %all-to-all-start = ((f16[16,328,128]{2,1,0:T(8,128)(2,1)}), f16[16,328,128]{2,1,0:T(8,128)(2,1)S(1)}, u32[]{:S(2)}, u32[]{:S(2)}) async-start(f16[16,328,128]{2,1,0:T(8,128)(2,1)} %broadcast_in_dim.3), calls=%async_computation | async-start | bytes 2686976 | tf_op jit(solution)/shard_map/all_to_all | solution.py:313
  14.3 14.7 %collective-permute-start = (bf16[160,5120]{1,0:T(8,128)(2,1)}, bf16[160,5120]{1,0:T(8,128)(2,1)S(1)}, u32[]{:S(2)}, u32[]{:S(2)}) collective-permute-start(bf16[160,5120]{1,0:T(8,128)(2,1)} %get-tuple-element.11), channel_id=1, source_target_pairs={{0,16},{16,0},{1,17},{17,1},{2,18},{18,2},{3,19},{19,3},{4,20},{20... | collective-permute-start | bytes 4915208 | tf_op jit(solution)/shard_map/ppermute | solution.py:324
  29.0 6.7 %copy-start = (bf16[160,5120]{1,0:T(8,128)(2,1)S(1)}, bf16[160,5120]{1,0:T(8,128)(2,1)}, u32[]{:S(2)}) copy-start(bf16[160,5120]{1,0:T(8,128)(2,1)} %get-tuple-element.10.rows_ref) | copy-start | bytes 4915204

commit v6 on v5

--- a/solution.py
+++ b/solution.py
@@ -112,12 +112,13 @@
         one.wait()
 
 
-def decode_kernel(values_ref, factor_ref):
+def decode_kernel(values_ref, factor_ref, *, ny):
     chunks, tall, both = values_ref.shape
     local = tall - EXTRA
-    for f in range(chunks):
-        scale = jnp.exp2(values_ref[f, pl.ds(local, 1), :] - LIFT)
-        value = values_ref[f, pl.ds(0, local), :] * scale
+    for g in range(chunks):
+        f = (g % ny) * (chunks // ny) + g // ny
+        scale = jnp.exp2(values_ref[g, pl.ds(local, 1), :] - LIFT)
+        value = values_ref[g, pl.ds(0, local), :] * scale
         high = value.astype(jnp.bfloat16)
         factor_ref[pl.ds(f * local, local), pl.ds(0, both)] = high
         low = value - high.astype(jnp.float32)
@@ -172,7 +173,7 @@
     scale = scale_of(values)
     lane = lax.broadcasted_iota(jnp.int32, (half, 2 * half), 1)
     up = jnp.where(lane < half, product[:half] * scale, 0.0).astype(jnp.bfloat16)
-    turned = stacked(of_g, of_x)
+    turned = product.T
     down = jnp.where(lane < half, 0.0, turned[half:] * scale).astype(jnp.bfloat16)
     features_ref[...] = jnp.concatenate([paired(up, False), paired(down, True)], axis=0)
     rounded = (values * scale).astype(jnp.bfloat16)
@@ -310,7 +311,7 @@
         ))
     )
     blocks = jnp.broadcast_to(block.astype(jnp.float16), (ny * nx, tall, both))
-    gathered = lax.all_to_all(blocks, ("y", "x"), 0, 0)
+    gathered = lax.all_to_all(blocks, ("x", "y"), 0, 0)
     keep, send = pl.pallas_call(
         pick_kernel,
         out_shape=(shape((tokens + held_rows, width), bf16),) * 2,
@@ -324,7 +325,7 @@
     recv = lax.ppermute(send, "c", swap)
 
     factor = pl.pallas_call(
-        decode_kernel,
+        functools.partial(decode_kernel, ny=ny),
         out_shape=shape((width, 2 * both), bf16),
         in_specs=[VMEM],
         out_specs=VMEM,

time: 89.8 us -> 89.9 us (level)
  no operation moved by 1% of the time
where the time goes in v6:
time: 89.9 us; the launch traced here: 89.6 us
  blocking collectives  57.8 us (64%)
  starting transfers between devices  12.5 us (14%)
  waiting for transfers between devices  8.55 us (10%)
  Pallas kernels  8.52 us (9%)
  local copies, waits for them, and re-layouts  1.25 us (1%)
    all_to_all x1, blocking collectives, shards(): held_every = lax.all_to_all(to_z, 'z', 0, 0)  26.9 us
    all_to_all x1, blocking collectives, shards(): in_plane = lax.all_to_all(to_plane, PLANE, 0, 0)  12.7 us
    all_to_all x1, blocking collectives, shards(): back = lax.all_to_all(partial, PLANE, 0, 0)  12.3 us
    all_to_all x1, waiting for transfers between devices, shards(): gathered = lax.all_to_all(blocks, ('x', 'y'), 0, 0)  8.54 us
    all_to_all x1, starting transfers between devices, shards(): gathered = lax.all_to_all(blocks, ('x', 'y'), 0, 0)  7.58 us
    all_gather x1, blocking collectives, shards(): pair = lax.all_gather(other, 'c')  5.96 us
    ppermute x1, starting transfers between devices, shards(): recv = lax.ppermute(send, 'c', swap)  4.9 us
    pallas_call x1, Pallas kernels, shards(): pl.pallas_call(pick_kernel, out_shape=(shape((tokens + held_rows, width),...  3.59 us
  transfers between devices with their start and end apart: 2, of which 1 were waited for; matrix products, arithmetic and copies ran while one was open for 0% of the time, Pallas kernels for 5%

profile of v6, /device:TPU:1, one launch (start us, length us, event | category | flops | bytes accessed | tf_op | source)
XLA Modules:
  0.0 89.6 jit_solution(7986501013181556179)
XLA Ops:
  0.6 1.2 %prepare.1 = f32[328,128]{1,0:T(8,128)S(1)} custom-call(bf16[320,128]{1,0:T(8,128)(2,1)} %down_ref.1, bf16[320,128]{1,0:T(8,128)(2,1)} %bitcast.17, bf16[64,128]{1,0:T(8,128)(2,1)} %bitcast.20, bf16[64,128]{1,0:T(8,128)(2,1)} %bitcast.21, bf16[64,320]{1,0:T(8,128)(2,1)} %bitcast.18, bf16[64,320]{1,0:T(8,128)(2,1)} %bitcast.19), custom_call_target="tpu_custom_call" | custom-call | tf_op jit(solution)/shard_map/prepare/pallas_call | solution.py:294
  1.8 1.2 %broadcast_in_dim.3 = f16[16,328,128]{2,1,0:T(8,128)(2,1)} broadcast(f16[328,128]{1,0:T(8,128)(2,1)S(1)} %convert_element_type.6), dimensions={1,2} | broadcast | bytes 1427456 | tf_op jit(solution)/shard_map/broadcast_in_dim | solution.py:313
  3.1 7.6 %all-to-all-start = ((f16[16,328,128]{2,1,0:T(8,128)(2,1)}), f16[16,328,128]{2,1,0:T(8,128)(2,1)S(1)}, u32[]{:S(2)}, u32[]{:S(2)}) async-start(f16[16,328,128]{2,1,0:T(8,128)(2,1)} %broadcast_in_dim.3), calls=%async_computation | async-start | bytes 2686976 | tf_op jit(solution)/shard_map/all_to_all | solution.py:314
  10.7 3.6 %pick.1 = (bf16[160,5120]{1,0:T(8,128)(2,1)}, bf16[160,5120]{1,0:T(8,128)(2,1)}) custom-call(bf16[128,5120]{1,0:T(8,128)(2,1)} %bitcast.13, bf16[128,5120]{1,0:T(8,128)(2,1)} %bitcast.14, bf16[32,5120]{1,0:T(8,128)(2,1)} %bitcast.15, bf16[32,5120]{1,0:T(8,128)(2,1)} %bitcast.16), custom_call_target="tpu_custom_call" | custom-call | tf_op jit(solution)/shard_map/pick/pallas_call | solution.py:315
  14.3 4.9 %collective-permute-start = (bf16[160,5120]{1,0:T(8,128)(2,1)}, bf16[160,5120]{1,0:T(8,128)(2,1)S(1)}, u32[]{:S(2)}, u32[]{:S(2)}) collective-permute-start(bf16[160,5120]{1,0:T(8,128)(2,1)} %get-tuple-element.11), channel_id=1, source_target_pairs={{0,16},{16,0},{1,17},{17,1},{2,18},{18,2},{3,19},{19,3},{4,20},{20... | collective-permute-start | bytes 4915208 | tf_op jit(solution)/shard_map/ppermute | solution.py:325
  19.2 8.5 %all-to-all-done = f16[16,328,128]{2,1,0:T(8,128)(2,1)S(1)} async-done(((f16[16,328,128]{2,1,0:T(8,128)(2,1)}), f16[16,328,128]{2,1,0:T(8,128)(2,1)S(1)}, u32[]{:S(2)}, u32[]{:S(2)}) %all-to-all-start) | async-done | bytes 1343520 | tf_op jit(solution)/shard_map/all_to_all | solution.py:314
  27.7 0.2 convert_element_type.7.values_ref
  27.9 0.6 decode.1.factor_ref
  28.4 0.0 copy-start
  28.5 0.0 collective-permute-done.rows_ref
  28.5 0.6 products.2
  29.1 6.0 %all-gather = f32[256,128]{1,0:T(8,128)S(1)} all-gather(f32[128,128]{1,0:T(8,128)S(1)} %get-tuple-element.14), channel_id=2, replica_groups=mesh['z'=16,'c'=2,'y'=4,'x'=4] {'c'}, dimensions={0}, use_global_device_ids=true | all-gather | bytes 196608 | tf_op jit(solution)/shard_map/all_gather | solution.py:348
  35.0 0.0 copy-done
  35.0 0.6 products.3
  35.6 0.6 spread.1
  36.2 12.7 %all_to_all.20.tokens_ref = bf16[32,32,128]{2,1,0:T(8,128)(2,1)S(1)} all-to-all(bf16[32,32,128]{2,1,0:T(8,128)(2,1)S(1)} %get-tuple-element.16), channel_id=1, replica_groups=mesh['z'=16,'c'=2,'y'=4,'x'=4] {'y','x','c'}, dimensions={0} | all-to-all | bytes 524288 | tf_op jit(solution)/shard_map/all_to_all | solution.py:358
  48.9 0.3 held_features.1
  49.3 26.9 %all_to_all.21 = bf16[16,16,128]{2,1,0:T(8,128)(2,1)S(1)} all-to-all(bf16[16,16,128]{2,1,0:T(8,128)(2,1)S(1)} %held_features.1), channel_id=1, replica_groups=mesh['z'=16,'c'=2,'y'=4,'x'=4] {'z'}, dimensions={0} | all-to-all | bytes 131072 | tf_op jit(solution)/shard_map/all_to_all | solution.py:369
  76.1 0.5 partial_influence.1
  76.6 12.3 %all_to_all.22.back_ref = f32[32,1,128]{2,1,0:T(1,128)S(1)} all-to-all(f32[32,1,128]{2,1,0:T(1,128)S(1)} %partial_influence.1), channel_id=1, replica_groups=mesh['z'=16,'c'=2,'y'=4,'x'=4] {'y','x','c'}, dimensions={0} | all-to-all | bytes 32768 | tf_op jit(solution)/shard_map/all_to_all | solution.py:379
  88.9 0.7 final.1
  (1 shorter events, 0.0 us)
Async XLA Ops:
  3.1 24.6 %all-to-all-start = ((f16[16,328,128]{2,1,0:T(8,128)(2,1)}), f16[16,328,128]{2,1,0:T(8,128)(2,1)S(1)}, u32[]{:S(2)}, u32[]{:S(2)}) async-start(f16[16,328,128]{2,1,0:T(8,128)(2,1)} %broadcast_in_dim.3), calls=%async_computation | async-start | bytes 2686976 | tf_op jit(solution)/shard_map/all_to_all | solution.py:314
  14.3 14.2 %collective-permute-start = (bf16[160,5120]{1,0:T(8,128)(2,1)}, bf16[160,5120]{1,0:T(8,128)(2,1)S(1)}, u32[]{:S(2)}, u32[]{:S(2)}) collective-permute-start(bf16[160,5120]{1,0:T(8,128)(2,1)} %get-tuple-element.11), channel_id=1, source_target_pairs={{0,16},{16,0},{1,17},{17,1},{2,18},{18,2},{3,19},{19,3},{4,20},{20... | collective-permute-start | bytes 4915208 | tf_op jit(solution)/shard_map/ppermute | solution.py:325
  28.4 6.6 %copy-start = (bf16[160,5120]{1,0:T(8,128)(2,1)S(1)}, bf16[160,5120]{1,0:T(8,128)(2,1)}, u32[]{:S(2)}) copy-start(bf16[160,5120]{1,0:T(8,128)(2,1)} %get-tuple-element.10.rows_ref) | copy-start | bytes 4915204

commit v7 on v5

--- a/solution.py
+++ b/solution.py
@@ -68,16 +68,15 @@
     mine = rank[...]
     folded = nt(
         adapter[...],
-        jnp.concatenate([jnp.where(first, blank, mine), jnp.where(first, mine, blank)], axis=0),
+        jnp.concatenate([blank, mine], axis=0),
     )
     signs = wide[...].astype(jnp.float32)
     blank = jnp.zeros_like(signs)
-    signs = jnp.concatenate([jnp.where(first, signs, blank), jnp.where(first, blank, signs)], axis=0)
+    signs = jnp.concatenate([signs, blank], axis=0)
     top = jnp.max(jnp.abs(folded), axis=0, keepdims=True)
     exponent = jnp.floor(jnp.log2(jnp.maximum(top, 2.0**-100)))
     lane = lax.broadcasted_iota(jnp.int32, (1, 2 * half), 1)
-    is_folded = (lane >= half) == first
-    exponent = jnp.where(is_folded, exponent, LIFT)
+    exponent = jnp.where(lane >= half, exponent, LIFT)
     block_ref[pl.ds(0, rows), :] = folded * jnp.exp2(LIFT - exponent) + signs.T
     block_ref[pl.ds(rows, EXTRA), :] = jnp.broadcast_to(exponent, (EXTRA, 2 * half))
 
@@ -149,7 +148,7 @@
 
 def joined(product, half):
     lane = lax.broadcasted_iota(jnp.int32, (half, 2 * half), 1)
-    return jnp.where(lane < half, product[:half], product[half:])
+    return jnp.where(lane < half, product[half:], product[:half])
 
 
 def scale_of(values):
@@ -171,10 +170,10 @@
     values = joined(product, half)
     scale = scale_of(values)
     lane = lax.broadcasted_iota(jnp.int32, (half, 2 * half), 1)
-    up = jnp.where(lane < half, product[:half] * scale, 0.0).astype(jnp.bfloat16)
+    up = jnp.where(lane < half, product[half:] * scale, 0.0).astype(jnp.bfloat16)
     turned = stacked(of_g, of_x)
-    down = jnp.where(lane < half, 0.0, turned[half:] * scale).astype(jnp.bfloat16)
-    features_ref[...] = jnp.concatenate([paired(up, False), paired(down, True)], axis=0)
+    down = jnp.where(lane < half, turned[half:] * scale, 0.0).astype(jnp.bfloat16)
+    features_ref[...] = jnp.concatenate([paired(up, False), paired(down, False)], axis=0)
     rounded = (values * scale).astype(jnp.bfloat16)
     rows = half // copies
     groups = out_ref.shape[0] // (2 * copies)

time: 89.8 us -> 89.8 us (level)
  no operation moved by 1% of the time
where the time goes in v7:
time: 89.8 us; the launch traced here: 89.4 us
  blocking collectives  57.1 us (64%)
  starting transfers between devices  12.5 us (14%)
  waiting for transfers between devices  9.07 us (10%)
  Pallas kernels  8.52 us (9%)
  local copies, waits for them, and re-layouts  1.25 us (1%)
    all_to_all x1, blocking collectives, shards(): held_every = lax.all_to_all(to_z, 'z', 0, 0)  26.8 us
    all_to_all x1, blocking collectives, shards(): back = lax.all_to_all(partial, PLANE, 0, 0)  12.3 us
    all_to_all x1, blocking collectives, shards(): in_plane = lax.all_to_all(to_plane, PLANE, 0, 0)  12 us
    all_to_all x1, waiting for transfers between devices, shards(): gathered = lax.all_to_all(blocks, ('y', 'x'), 0, 0)  9.07 us
    all_to_all x1, starting transfers between devices, shards(): gathered = lax.all_to_all(blocks, ('y', 'x'), 0, 0)  7.58 us
    all_gather x1, blocking collectives, shards(): pair = lax.all_gather(other, 'c')  6.03 us
    ppermute x1, starting transfers between devices, shards(): recv = lax.ppermute(send, 'c', swap)  4.9 us
    pallas_call x1, Pallas kernels, shards(): pl.pallas_call(pick_kernel, out_shape=(shape((tokens + held_rows, width),...  3.59 us
  transfers between devices with their start and end apart: 2, of which 1 were waited for; matrix products, arithmetic and copies ran while one was open for 0% of the time, Pallas kernels for 5%

profile of v7, /device:TPU:1, one launch (start us, length us, event | category | flops | bytes accessed | tf_op | source)
XLA Modules:
  0.0 89.4 jit_solution(3268945187924952443)
XLA Ops:
  0.6 1.1 %prepare.1 = f32[328,128]{1,0:T(8,128)S(1)} custom-call(bf16[320,128]{1,0:T(8,128)(2,1)} %down_ref.1, bf16[320,128]{1,0:T(8,128)(2,1)} %bitcast.17, bf16[64,128]{1,0:T(8,128)(2,1)} %bitcast.20, bf16[64,128]{1,0:T(8,128)(2,1)} %bitcast.21, bf16[64,320]{1,0:T(8,128)(2,1)} %bitcast.18, bf16[64,320]{1,0:T(8,128)(2,1)} %bitcast.19), custom_call_target="tpu_custom_call" | custom-call | tf_op jit(solution)/shard_map/prepare/pallas_call | solution.py:292
  1.8 1.2 %broadcast_in_dim.3 = f16[16,328,128]{2,1,0:T(8,128)(2,1)} broadcast(f16[328,128]{1,0:T(8,128)(2,1)S(1)} %convert_element_type.6), dimensions={1,2} | broadcast | bytes 1427456 | tf_op jit(solution)/shard_map/broadcast_in_dim | solution.py:311
  3.1 7.6 %all-to-all-start = ((f16[16,328,128]{2,1,0:T(8,128)(2,1)}), f16[16,328,128]{2,1,0:T(8,128)(2,1)S(1)}, u32[]{:S(2)}, u32[]{:S(2)}) async-start(f16[16,328,128]{2,1,0:T(8,128)(2,1)} %broadcast_in_dim.3), calls=%async_computation | async-start | bytes 2686976 | tf_op jit(solution)/shard_map/all_to_all | solution.py:312
  10.6 3.6 %pick.1 = (bf16[160,5120]{1,0:T(8,128)(2,1)}, bf16[160,5120]{1,0:T(8,128)(2,1)}) custom-call(bf16[128,5120]{1,0:T(8,128)(2,1)} %bitcast.13, bf16[128,5120]{1,0:T(8,128)(2,1)} %bitcast.14, bf16[32,5120]{1,0:T(8,128)(2,1)} %bitcast.15, bf16[32,5120]{1,0:T(8,128)(2,1)} %bitcast.16), custom_call_target="tpu_custom_call" | custom-call | tf_op jit(solution)/shard_map/pick/pallas_call | solution.py:313
  14.2 4.9 %collective-permute-start = (bf16[160,5120]{1,0:T(8,128)(2,1)}, bf16[160,5120]{1,0:T(8,128)(2,1)S(1)}, u32[]{:S(2)}, u32[]{:S(2)}) collective-permute-start(bf16[160,5120]{1,0:T(8,128)(2,1)} %get-tuple-element.11), channel_id=1, source_target_pairs={{0,16},{16,0},{1,17},{17,1},{2,18},{18,2},{3,19},{19,3},{4,20},{20... | collective-permute-start | bytes 4915208 | tf_op jit(solution)/shard_map/ppermute | solution.py:323
  19.2 9.1 %all-to-all-done = f16[16,328,128]{2,1,0:T(8,128)(2,1)S(1)} async-done(((f16[16,328,128]{2,1,0:T(8,128)(2,1)}), f16[16,328,128]{2,1,0:T(8,128)(2,1)S(1)}, u32[]{:S(2)}, u32[]{:S(2)}) %all-to-all-start) | async-done | bytes 1343520 | tf_op jit(solution)/shard_map/all_to_all | solution.py:312
  28.2 0.2 convert_element_type.7.values_ref
  28.4 0.6 decode.1.factor_ref
  29.0 0.0 copy-start
  29.0 0.0 collective-permute-done.rows_ref
  29.0 0.6 products.2
  29.6 6.0 %all-gather = f32[256,128]{1,0:T(8,128)S(1)} all-gather(f32[128,128]{1,0:T(8,128)S(1)} %get-tuple-element.14), channel_id=2, replica_groups=mesh['z'=16,'c'=2,'y'=4,'x'=4] {'c'}, dimensions={0}, use_global_device_ids=true | all-gather | bytes 196608 | tf_op jit(solution)/shard_map/all_gather | solution.py:346
  35.6 0.0 copy-done
  35.6 0.6 products.3
  36.2 0.6 spread.1
  36.8 12.0 %all_to_all.20.tokens_ref = bf16[32,32,128]{2,1,0:T(8,128)(2,1)S(1)} all-to-all(bf16[32,32,128]{2,1,0:T(8,128)(2,1)S(1)} %get-tuple-element.16), channel_id=1, replica_groups=mesh['z'=16,'c'=2,'y'=4,'x'=4] {'y','x','c'}, dimensions={0} | all-to-all | bytes 524288 | tf_op jit(solution)/shard_map/all_to_all | solution.py:356
  48.8 0.3 held_features.1
  49.1 26.8 %all_to_all.21 = bf16[16,16,128]{2,1,0:T(8,128)(2,1)S(1)} all-to-all(bf16[16,16,128]{2,1,0:T(8,128)(2,1)S(1)} %held_features.1), channel_id=1, replica_groups=mesh['z'=16,'c'=2,'y'=4,'x'=4] {'z'}, dimensions={0} | all-to-all | bytes 131072 | tf_op jit(solution)/shard_map/all_to_all | solution.py:367
  76.0 0.5 partial_influence.1
  76.4 12.3 %all_to_all.22.back_ref = f32[32,1,128]{2,1,0:T(1,128)S(1)} all-to-all(f32[32,1,128]{2,1,0:T(1,128)S(1)} %partial_influence.1), channel_id=1, replica_groups=mesh['z'=16,'c'=2,'y'=4,'x'=4] {'y','x','c'}, dimensions={0} | all-to-all | bytes 32768 | tf_op jit(solution)/shard_map/all_to_all | solution.py:377
  88.7 0.7 final.1
  (1 shorter events, 0.0 us)
Async XLA Ops:
  3.1 25.2 %all-to-all-start = ((f16[16,328,128]{2,1,0:T(8,128)(2,1)}), f16[16,328,128]{2,1,0:T(8,128)(2,1)S(1)}, u32[]{:S(2)}, u32[]{:S(2)}) async-start(f16[16,328,128]{2,1,0:T(8,128)(2,1)} %broadcast_in_dim.3), calls=%async_computation | async-start | bytes 2686976 | tf_op jit(solution)/shard_map/all_to_all | solution.py:312
  14.2 14.7 %collective-permute-start = (bf16[160,5120]{1,0:T(8,128)(2,1)}, bf16[160,5120]{1,0:T(8,128)(2,1)S(1)}, u32[]{:S(2)}, u32[]{:S(2)}) collective-permute-start(bf16[160,5120]{1,0:T(8,128)(2,1)} %get-tuple-element.11), channel_id=1, source_target_pairs={{0,16},{16,0},{1,17},{17,1},{2,18},{18,2},{3,19},{19,3},{4,20},{20... | collective-permute-start | bytes 4915208 | tf_op jit(solution)/shard_map/ppermute | solution.py:323
  29.0 6.7 %copy-start = (bf16[160,5120]{1,0:T(8,128)(2,1)S(1)}, bf16[160,5120]{1,0:T(8,128)(2,1)}, u32[]{:S(2)}) copy-start(bf16[160,5120]{1,0:T(8,128)(2,1)} %get-tuple-element.10.rows_ref) | copy-start | bytes 4915204
